TPU v7x, 256 devices: a whole 4x4x8 slice. The times are simulated.
256 devices in a mesh: row: 16 (over z, y_lo), col: 4 (over x), ch: 4 (over y_hi, core).
Axes of the slice: x: 4, y: 4 (y_hi: 2, y_lo: 2; y = y_hi * 2 + y_lo), z: 8, core: 2. Of those that a mesh axis runs over, the one named last changes fastest.
Arguments:
- pair: float32 [1024, 1024, 128], P('row', ('col', 'ch')), may hold values from -30 to 30
- token_mask: int32 [1024], replicated, may hold values 0 or 1
- in_gain: float32 [2, 128], replicated, may hold values from 0.1 to 1.9
- in_bias: float32 [2, 128], replicated, may hold values from -3 to 3
- proj_weight: bfloat16 [2, 128, 512], replicated, may hold values from -0.5 to 0.5
- gate_weight: bfloat16 [2, 128, 128], replicated, may hold values from -0.5 to 0.5
- mid_gain: float32 [2, 128], replicated, may hold values from 0.1 to 1.9
- mid_bias: float32 [2, 128], replicated, may hold values from -3 to 3
- out_weight: bfloat16 [2, 128, 128], replicated, may hold values from -0.5 to 0.5
Outputs:
- new_pair: float32 [1024, 1024, 128], P('row', ('col', 'ch'))
All inputs are finite; a program needn't handle non-finite values.
Results may differ from a plain program's by a relative error of at most 0.0022.
Values may be sent and summed in bfloat16 or wider, within the bound.
No kernel may reach another device: no remote copies, remote signals or barrier semaphores. Data moves between devices by JAX's collectives and lax.ppermute only.
A program may use at most 192 MiB of HBM per device.

v0:
```python
import jax
import jax.numpy as jnp
from jax import lax
from jax.sharding import PartitionSpec as P


def layer_norm(values, scale_by, shift_by, along):
    average = jnp.mean(values, axis=along, keepdims=True)
    centred = values - average
    spread = jnp.mean(centred * centred, axis=along, keepdims=True)
    return centred * lax.rsqrt(spread + 1e-05) * scale_by + shift_by


def outgoing(left_block, right_block):
    partial_sums = jnp.einsum(
        "cik,cjk->cij",
        left_block,
        lax.all_gather(right_block, "row", axis=1, tiled=True),
        preferred_element_type=jnp.float32,
    )
    return lax.psum_scatter(
        partial_sums.astype(jnp.bfloat16), "col", scatter_dimension=2, tiled=True
    ).astype(jnp.float32)


def incoming(left_block, right_block):
    all_left = lax.all_gather(left_block, "col", axis=2, tiled=True)
    left_cols = lax.all_to_all(all_left, "row", split_axis=2, concat_axis=1, tiled=True)
    return jnp.einsum(
        "cki,ckj->cij",
        left_cols,
        lax.all_gather(right_block, "row", axis=1, tiled=True),
        preferred_element_type=jnp.float32,
    )


def on_device(
    pair, token_mask, in_gain, in_bias, proj_weight, gate_weight, mid_gain, mid_bias, out_weight
):
    tile_rows = pair.shape[0]
    tile_cols = pair.shape[1]
    channels = pair.shape[2]
    slice_width = channels // lax.axis_size("ch")
    row_index = lax.axis_index("row")
    col_index = lax.axis_index("col") * lax.axis_size("ch") + lax.axis_index("ch")
    slice_start = lax.axis_index("ch") * slice_width
    row_mask = lax.dynamic_slice_in_dim(token_mask, row_index * tile_rows, tile_rows).astype(
        jnp.float32
    )
    col_mask = lax.dynamic_slice_in_dim(token_mask, col_index * tile_cols, tile_cols).astype(
        jnp.float32
    )
    pair_mask = row_mask[:, None] * col_mask[None, :]
    current = pair
    for section in range(2):
        normed = layer_norm(current, in_gain[section], in_bias[section], 2).astype(jnp.bfloat16)
        projected = jnp.einsum(
            "ijc,cd->dij", normed, proj_weight[section], preferred_element_type=jnp.float32
        )
        left_block = (
            jax.nn.sigmoid(projected[:channels])
            * projected[channels : 2 * channels]
            * pair_mask[None]
        ).astype(jnp.bfloat16)
        right_block = (
            jax.nn.sigmoid(projected[2 * channels : 3 * channels])
            * projected[3 * channels :]
            * pair_mask[None]
        ).astype(jnp.bfloat16)
        gate_values = jax.nn.sigmoid(
            jnp.einsum(
                "ijc,cd->ijd", normed, gate_weight[section], preferred_element_type=jnp.float32
            )
        )
        left_block, right_block = (
            lax.all_to_all(left_block, "ch", split_axis=0, concat_axis=2, tiled=True),
            lax.all_to_all(right_block, "ch", split_axis=0, concat_axis=2, tiled=True),
        )
        if section == 0:
            triangle = outgoing(left_block, right_block)
        else:
            triangle = incoming(left_block, right_block)
        average = (
            lax.psum(jnp.sum(triangle, axis=0).astype(jnp.bfloat16), "ch").astype(jnp.float32)
            / channels
        )
        centred = triangle - average[None]
        spread = (
            lax.psum(jnp.sum(centred * centred, axis=0).astype(jnp.bfloat16), "ch").astype(
                jnp.float32
            )
            / channels
        )
        gains = lax.dynamic_slice_in_dim(mid_gain[section], slice_start, slice_width)
        offsets = lax.dynamic_slice_in_dim(mid_bias[section], slice_start, slice_width)
        normed_mid = (
            centred * lax.rsqrt(spread + 1e-05)[None] * gains[:, None, None]
            + offsets[:, None, None]
        ).astype(jnp.bfloat16)
        normed_mid = lax.all_to_all(normed_mid, "ch", split_axis=2, concat_axis=0, tiled=True)
        update_values = jnp.einsum(
            "cij,cd->ijd", normed_mid, out_weight[section], preferred_element_type=jnp.float32
        )
        current = current + gate_values * update_values
    return current


def solution(mesh):
    return jax.shard_map(
        on_device,
        mesh=mesh,
        in_specs=(P("row", ("col", "ch"), None), P(), P(), P(), P(), P(), P(), P(), P()),
        out_specs=P("row", ("col", "ch"), None),
        check_vma=False,
    )
```

profile of v0, /device:TPU:32, one launch (start us, length us, event | category | flops | bytes accessed | tf_op | source)
XLA Modules:
  0.0 1143.8 jit_solution(4520000665239013881)
XLA Ops:
  14.6 4.6 copy.30
  23.6 20.5 %all_to_all.126 = bf16[4,2,65536]{2,1,0:T(2,128)(2,1)} all-to-all(bf16[4,2,65536]{2,1,0:T(2,128)(2,1)} %reshape.79), channel_id=1, replica_groups=mesh['row'=16,'col'=4,'ch'=4] {'ch'}, dimensions={0} | all-to-all | bytes 2097152 | tf_op jit(solution)/shard_map/all_to_all | solution.py:77
  48.4 4.9 copy.31
  64.8 50.2 %all_to_all.127 = bf16[4,2,65536]{2,1,0:T(2,128)(2,1)} all-to-all(bf16[4,2,65536]{2,1,0:T(2,128)(2,1)S(1)} %reshape.77), channel_id=1, replica_groups=mesh['row'=16,'col'=4,'ch'=4] {'ch'}, dimensions={0} | all-to-all | bytes 2097152 | tf_op jit(solution)/shard_map/all_to_all | solution.py:76
  119.3 4.9 copy.29
  127.7 295.5 %all-gather.4.cloned.1.call-done = bf16[32,1024,256]{2,1,0:T(8,128)(2,1)} async-done(((bf16[32,64,256]{2,1,0:T(8,128)(2,1)}), bf16[32,1024,256]{2,1,0:T(8,128)(2,1)}) %all-gather.4.cloned.1.call-update) | async-done | bytes 16777232 | tf_op jit(solution)/shard_map/all_gather | solution.py:18
  423.1 9.9 convolution_convert_fusion
  433.9 51.8 %reduce-scatter.2.cloned.1.call-done = bf16[32,64,256]{2,1,0:T(8,128)(2,1)} async-done(((bf16[32,64,1024]{2,1,0:T(8,128)(2,1)}), bf16[32,64,256]{2,1,0:T(8,128)(2,1)}) %reduce-scatter.2.cloned.1.call-update) | async-done | bytes 1048592 | tf_op jit(solution)/shard_map/reduce_scatter | solution.py:21
  487.1 15.9 %psum.28 = bf16[64,256]{1,0:T(8,128)(2,1)S(1)} all-reduce(bf16[64,256]{1,0:T(8,128)(2,1)S(1)} %reduce_sum.77), channel_id=1, replica_groups=mesh['row'=16,'col'=4,'ch'=4] {'ch'}, use_global_device_ids=true, to_apply=%region_4.0 | all-reduce | flops 16384 | bytes 65536 | tf_op jit(solution)/shard_map/psum | solution.py:84
  504.6 13.4 %psum.29 = bf16[64,256]{1,0:T(8,128)(2,1)S(1)} all-reduce(bf16[64,256]{1,0:T(8,128)(2,1)S(1)} %multiply_reduce_fusion.2), channel_id=1, replica_groups=mesh['row'=16,'col'=4,'ch'=4] {'ch'}, use_global_device_ids=true, to_apply=%region_6.0 | all-reduce | flops 16384 | bytes 65536 | tf_op jit(solution)/shard_map/psum | solution.py:89
  519.4 4.6 copy.32
  534.9 13.0 %all-to-all-done.2 = bf16[4,2,65536]{2,1,0:T(2,128)(2,1)S(1)} async-done(((bf16[4,2,65536]{2,1,0:T(2,128)(2,1)}), bf16[4,2,65536]{2,1,0:T(2,128)(2,1)S(1)}, u32[]{:S(2)}, u32[]{:S(2)}) %all-to-all-start.2) | async-done | bytes 1048608 | tf_op jit(solution)/shard_map/all_to_all | solution.py:100
  550.6 4.8 copy.33
  555.4 4.8 fusion.48
  571.5 20.5 %all_to_all.128 = bf16[4,2,65536]{2,1,0:T(2,128)(2,1)} all-to-all(bf16[4,2,65536]{2,1,0:T(2,128)(2,1)} %reshape.83), channel_id=1, replica_groups=mesh['row'=16,'col'=4,'ch'=4] {'ch'}, dimensions={0} | all-to-all | bytes 2097152 | tf_op jit(solution)/shard_map/all_to_all | solution.py:76
  607.4 19.1 %all_to_all.129 = bf16[4,2,65536]{2,1,0:T(2,128)(2,1)} all-to-all(bf16[4,2,65536]{2,1,0:T(2,128)(2,1)S(1)} %reshape.87), channel_id=1, replica_groups=mesh['row'=16,'col'=4,'ch'=4] {'ch'}, dimensions={0} | all-to-all | bytes 2097152 | tf_op jit(solution)/shard_map/all_to_all | solution.py:77
  637.3 17.4 %all-gather.6.cloned.1.call-done = bf16[32,64,1024]{2,1,0:T(8,128)(2,1)} async-done(((bf16[32,64,256]{2,1,0:T(8,128)(2,1)}), bf16[32,64,1024]{2,1,0:T(8,128)(2,1)}) %all-gather.6.cloned.1.call-update) | async-done | bytes 4194320 | tf_op jit(solution)/shard_map/all_gather | solution.py:27
  654.7 12.9 %copy.37 = bf16[32,64,1024]{1,0,2:T(8,128)(2,1)} copy(bf16[32,64,1024]{2,1,0:T(8,128)(2,1)} %all-gather.6.cloned.1.call-done) | data formatting | bytes 8388608 | tf_op jit(solution)/shard_map/all_gather | solution.py:27
  667.7 14.0 %reshape.85 = bf16[16,2,65536]{2,1,0:T(2,128)(2,1)} reshape(bf16[1024,32,64]{2,1,0:T(8,128)(2,1)} %bitcast.84) | data formatting | bytes 8388608
  681.7 8.8 all-to-all-start.4
  690.5 133.6 %all-to-all-done.4 = bf16[16,2,65536]{2,1,0:T(2,128)(2,1)} async-done(((bf16[16,2,65536]{2,1,0:T(2,128)(2,1)}), bf16[16,2,65536]{2,1,0:T(2,128)(2,1)}, u32[]{:S(2)}, u32[]{:S(2)}) %all-to-all-start.4) | async-done | bytes 4194336 | tf_op jit(solution)/shard_map/all_to_all | solution.py:28
  824.1 13.7 %reshape.86 = bf16[1024,32,64]{2,1,0:T(8,128)(2,1)} reshape(bf16[16,2,65536]{2,1,0:T(2,128)(2,1)} %all-to-all-done.4) | data formatting | bytes 8388608
  837.8 12.0 %copy.39 = bf16[32,16,64,64]{2,1,3,0:T(8,128)(2,1)} copy(bf16[32,16,64,64]{2,0,3,1:T(8,128)(2,1)} %bitcast.85) | data formatting | bytes 8388608 | tf_op jit(solution)/shard_map/all_to_all | solution.py:28
  849.8 11.9 %all_to_all.110 = bf16[32,1024,64]{1,2,0:T(8,128)(2,1)} reshape(bf16[32,16,64,64]{2,1,3,0:T(8,128)(2,1)} %copy.39) | data formatting | bytes 8388608 | tf_op jit(solution)/shard_map/all_to_all | solution.py:28
  861.6 192.1 %all-gather.8.cloned.1.call-done = bf16[32,1024,256]{2,1,0:T(8,128)(2,1)} async-done(((bf16[32,64,256]{2,1,0:T(8,128)(2,1)}), bf16[32,1024,256]{2,1,0:T(8,128)(2,1)}) %all-gather.8.cloned.1.call-update) | async-done | bytes 16777232 | tf_op jit(solution)/shard_map/all_gather | solution.py:32
  1053.7 9.7 fusion.49
  1063.5 17.6 %psum.30 = bf16[64,256]{1,0:T(8,128)(2,1)S(1)} all-reduce(bf16[64,256]{1,0:T(8,128)(2,1)S(1)} %get-tuple-element.21), channel_id=1, replica_groups=mesh['row'=16,'col'=4,'ch'=4] {'ch'}, use_global_device_ids=true, to_apply=%region_10.0 | all-reduce | flops 16384 | bytes 65536 | tf_op jit(solution)/shard_map/psum | solution.py:84
  1081.4 13.6 %psum.31 = bf16[64,256]{1,0:T(8,128)(2,1)S(1)} all-reduce(bf16[64,256]{1,0:T(8,128)(2,1)S(1)} %multiply_reduce_fusion), channel_id=1, replica_groups=mesh['row'=16,'col'=4,'ch'=4] {'ch'}, use_global_device_ids=true, to_apply=%region_12.0 | all-reduce | flops 16384 | bytes 65536 | tf_op jit(solution)/shard_map/psum | solution.py:89
  1099.2 4.6 reshape.89
  1109.8 13.5 %all-to-all-done.6 = bf16[4,2,65536]{2,1,0:T(2,128)(2,1)S(1)} async-done(((bf16[4,2,65536]{2,1,0:T(2,128)(2,1)}), bf16[4,2,65536]{2,1,0:T(2,128)(2,1)S(1)}, u32[]{:S(2)}, u32[]{:S(2)}) %all-to-all-start.6) | async-done | bytes 1048608 | tf_op jit(solution)/shard_map/all_to_all | solution.py:100
  1125.9 4.8 copy.43
  1130.7 6.1 multiply_add_fusion
  (84 shorter events, 105.3 us)
Async XLA Ops:
  6.5 2.4 copy-start
  6.5 416.6 %all-gather.4.cloned.1.call-start = ((), (), s32[]{:S(2)}) async-start(), calls=%async_computation.8 | async-start | bytes 17825792 | tf_op jit(solution)/shard_map/all_gather | solution.py:18
  6.5 4.6 copy-start.9
  6.5 4.6 copy-start.10
  6.5 4.7 copy-start.4
  57.6 428.0 %reduce-scatter.2.cloned.1.call-start = ((), (), s32[]{:S(2)}) async-start(), calls=%async_computation.9 | async-start | bytes 5242880 | tf_op jit(solution)/shard_map/reduce_scatter | solution.py:21
  433.1 0.7 copy-start.7
  433.1 0.7 copy-start.8
  485.7 32.3 %copy-start.3 = (bf16[32,64,256]{2,1,0:T(8,128)(2,1)S(1)}, bf16[32,64,256]{2,1,0:T(8,128)(2,1)}, u32[]{:S(2)}) copy-start(bf16[32,64,256]{2,1,0:T(8,128)(2,1)} %reduce-scatter.2.cloned.1.call-done) | copy-start | bytes 3145732
  524.0 8.4 copy-start.6
  528.5 19.5 %all-to-all-start.2 = ((bf16[4,2,65536]{2,1,0:T(2,128)(2,1)}), bf16[4,2,65536]{2,1,0:T(2,128)(2,1)S(1)}, u32[]{:S(2)}, u32[]{:S(2)}) async-start(bf16[4,2,65536]{2,1,0:T(2,128)(2,1)} %reshape.81), calls=%async_computation.3 | async-start | bytes 2097152 | tf_op jit(solution)/shard_map/all_to_all | solution.py:100
  532.0 122.8 %all-gather.6.cloned.1.call-start = ((), (), s32[]{:S(2)}) async-start(), calls=%async_computation.10 | async-start | bytes 5242880 | tf_op jit(solution)/shard_map/all_gather | solution.py:27
  550.6 4.8 copy-start.11
  560.2 2.7 copy-start.1
  560.2 1.4 copy-start.5
  602.7 451.0 %all-gather.8.cloned.1.call-start = ((), (), s32[]{:S(2)}) async-start(), calls=%async_computation.11 | async-start | bytes 17825792 | tf_op jit(solution)/shard_map/all_gather | solution.py:32
  681.7 142.5 %all-to-all-start.4 = ((bf16[16,2,65536]{2,1,0:T(2,128)(2,1)}), bf16[16,2,65536]{2,1,0:T(2,128)(2,1)}, u32[]{:S(2)}, u32[]{:S(2)}) async-start(bf16[16,2,65536]{2,1,0:T(2,128)(2,1)} %reshape.85), calls=%async_computation.5 | async-start | bytes 8388608 | tf_op jit(solution)/shard_map/all_to_all | solution.py:28
  1099.2 8.1 copy-start.2
  1103.8 19.5 %all-to-all-start.6 = ((bf16[4,2,65536]{2,1,0:T(2,128)(2,1)}), bf16[4,2,65536]{2,1,0:T(2,128)(2,1)S(1)}, u32[]{:S(2)}, u32[]{:S(2)}) async-start(bf16[4,2,65536]{2,1,0:T(2,128)(2,1)} %reshape.89), calls=%async_computation.7 | async-start | bytes 2097152 | tf_op jit(solution)/shard_map/all_to_all | solution.py:100
Sparse Core Ops, SparseCore 0:
  57.8 365.3 all-gather.3
  433.2 52.3 reduce-scatter.1
  602.8 51.8 all-gather.5
  656.5 397.1 all-gather.7
where the time goes:
time: 1160 us; the launch traced here: 1140 us
  waiting for transfers between devices  717 us (62%)
  local copies, waits for them, and re-layouts  173 us (15%)
  blocking collectives  171 us (15%)
  matrix products  38.1 us (3%)
  starting transfers between devices  16.3 us (1%)
  other arithmetic  15.1 us (1%)
  between operations  13.9 us (1%)
    all_gather x1, waiting for transfers between devices, outgoing(): lax.all_gather(right_block, 'row', axis=1, tiled=True)  295 us
    all_gather x1, waiting for transfers between devices, incoming(): lax.all_gather(right_block, 'row', axis=1, tiled=True)  192 us
    all_to_all x1, waiting for transfers between devices, incoming(): lax.all_to_all(all_left, 'row', split_axis=2, concat_axis=1, tiled=True)  134 us
    all_to_all x2, blocking collectives, on_device(): lax.all_to_all(left_block, 'ch', split_axis=0, concat_axis=2, tiled=True)  70.7 us
    unnamed x38, local copies, waits for them, and re-layouts  69.4 us
    reduce_scatter x1, waiting for transfers between devices, outgoing(): lax.psum_scatter(partial_sums.astype(jnp.bfloat16), 'col', scatter_dimens...  51.8 us
    all_to_all x2, blocking collectives, on_device(): lax.all_to_all(right_block, 'ch', split_axis=0, concat_axis=2, tiled=True)  39.6 us
    psum x2, blocking collectives, on_device(): lax.psum(jnp.sum(triangle, axis=0).astype(jnp.bfloat16), 'ch')  33.6 us
  transfers between devices with their start and end apart: 7, of which 7 were waited for; matrix products, arithmetic and copies ran while one was open for 7% of the time, Pallas kernels for 0%

commit v1 on v0

v1 whole, which is shorter than its diff:
```python
import jax
import jax.numpy as jnp
from jax import lax
from jax.experimental import pallas as pl
from jax.experimental.pallas import tpu as pltpu
from jax.sharding import PartitionSpec as P

F32 = jnp.float32
BF16 = jnp.bfloat16
C = 128
T = 64
H = 32
BLK = 16
VMEM_LIMIT = 40 * 1024 * 1024


def sigmoid(x):
    return 0.5 * jnp.tanh(0.5 * x) + 0.5


def layer_norm(values, gain, bias):
    average = jnp.mean(values, axis=-1, keepdims=True)
    centred = values - average
    spread = jnp.mean(centred * centred, axis=-1, keepdims=True)
    return centred * lax.rsqrt(spread + 1e-05) * gain + bias


def project_block(load, block, mask_ref, gain, bias, w_ref, g_ref, x_ref, gate_ref, sl_ref, sr_ref):
    for t in range(0, BLK, 2):
        s = block * BLK + t
        lines = jnp.concatenate([load(s), load(s + H), load(s + 1), load(s + 1 + H)], axis=0)
        normed = layer_norm(lines, gain, bias).astype(BF16)
        p = lax.dot_general(
            w_ref[...], normed, (((0,), (1,)), ((), ())), preferred_element_type=F32
        )
        gate = sigmoid(jnp.dot(normed, g_ref[...], preferred_element_type=F32))
        gate_ref[s] = gate[:C]
        gate_ref[s + 1] = gate[C:]
        left = sigmoid(p[:C]) * p[C : 2 * C]
        right = sigmoid(p[2 * C : 3 * C]) * p[3 * C :]
        for u in range(2):
            mask = mask_ref[pl.ds(s + u, 1), :]
            sl_ref[:, t + u, :] = left[:, u * C : (u + 1) * C] * mask
            sr_ref[:, t + u, :] = right[:, u * C : (u + 1) * C] * mask
    x_ref[:, pl.ds(pl.multiple_of(block * BLK, BLK), BLK), :] = sl_ref[...].astype(BF16)
    x_ref[:, pl.ds(pl.multiple_of(H + block * BLK, BLK), BLK), :] = sr_ref[...].astype(BF16)


def first_kernel(z_ref, mask_ref, gain_ref, bias_ref, w_ref, g_ref, x_ref, gate_ref, sl_ref, sr_ref):
    gain, bias = gain_ref[...], bias_ref[...]

    def body(block, carry):
        project_block(
            lambda s: z_ref[s], block, mask_ref, gain, bias, w_ref, g_ref, x_ref, gate_ref, sl_ref, sr_ref
        )
        return carry

    lax.fori_loop(0, H // BLK, body, 0)


def update_block(block, y_ref, gain, bias, ow_ref, gate_ref, s_ref, emit):
    y = y_ref[:, pl.ds(pl.multiple_of(block * BLK, BLK), BLK), :].astype(F32)
    average = jnp.sum(y, axis=0) * (1.0 / C)
    centred = y - average[None]
    spread = jnp.sum(centred * centred, axis=0) * (1.0 / C)
    s_ref[...] = centred * lax.rsqrt(spread + 1e-05)[None]
    for t in range(BLK):
        s = block * BLK + t
        normed = (s_ref[:, t, :] * gain + bias).astype(BF16)
        update = lax.dot_general(
            normed, ow_ref[...], (((0,), (0,)), ((), ())), preferred_element_type=F32
        )
        emit(s, gate_ref[s] * update)


def middle_kernel(
    y_ref, z_ref, gate0_ref, mgain_ref, mbias_ref, ow_ref, mask_ref, gain_ref, bias_ref, w_ref, g_ref,
    x_ref, gate_ref, zn_ref, sl_ref, sr_ref,
):
    mgain, mbias = mgain_ref[...], mbias_ref[...]
    gain, bias = gain_ref[...], bias_ref[...]

    def emit(s, change):
        zn_ref[s] = z_ref[s] + change[:T]
        zn_ref[s + H] = z_ref[s + H] + change[T:]

    def body(block, carry):
        update_block(block, y_ref, mgain, mbias, ow_ref, gate0_ref, sl_ref, emit)
        return carry

    lax.fori_loop(0, H // BLK, body, 0)

    for block in range(H // BLK):
        project_block(
            lambda s: zn_ref[:, s, :], block, mask_ref, gain, bias, w_ref, g_ref, x_ref, gate_ref, sl_ref, sr_ref
        )


def last_kernel(y_ref, z_ref, gate_ref, mgain_ref, mbias_ref, ow_ref, out_ref, s_ref):
    mgain, mbias = mgain_ref[...], mbias_ref[...]

    def emit(s, change):
        out_ref[:, s, :] = z_ref[:, s, :] + change[:T]
        out_ref[:, s + H, :] = z_ref[:, s + H, :] + change[T:]

    for block in range(H // BLK):
        update_block(block, y_ref, mgain, mbias, ow_ref, gate_ref, s_ref, emit)


def sides(x0, x1):
    low = jnp.concatenate([x0[:, :T], x1[:, :T]], axis=1)
    high = jnp.concatenate([x0[:, T:], x1[:, T:]], axis=1)
    return low, high


def nt_dot(a, b):
    return lax.dot_general(a, b, (((1,), (1,)), ((), ())), preferred_element_type=F32)


def outgoing_kernel(x_ref, l_ref, r_ref, other_ref, rs_ref):
    core = lax.axis_index("core")

    def gather(row, carry):
        at = pl.multiple_of(row * T, T)
        to = pl.multiple_of(lax.rem(row, 2) * 512 + lax.div(row, 2) * T, T)
        for q in range(4):
            low, high = sides(x_ref[row * 8 + 2 * q], x_ref[row * 8 + 2 * q + 1])
            cols = slice(q * 128, (q + 1) * 128)
            l_ref[pl.ds(at, H), cols] = low[:H]
            l_ref[pl.ds(at + H, H), cols] = high[:H]
            rs_ref[pl.ds(to, H), cols] = low[H:]
            rs_ref[pl.ds(to + H, H), cols] = high[H:]
        return carry

    lax.fori_loop(0, 16, gather, 0)
    r_ref[...] = rs_ref[pl.ds(pl.multiple_of(core * 512, 512), 512), :]
    send = rs_ref[pl.ds(pl.multiple_of((1 - core) * 512, 512), 512), :]

    def multiply(i, carry):
        rows = pl.ds(pl.multiple_of(i * 256, 256), 256)
        other_ref[rows, :] = nt_dot(l_ref[rows, :], send).astype(BF16)
        return carry

    lax.fori_loop(0, 4, multiply, 0)


def outgoing_sum_kernel(l_ref, r_ref, got_ref, y_ref):
    def body(i, carry):
        rows = pl.ds(pl.multiple_of(i * 256, 256), 256)
        total = (nt_dot(l_ref[rows, :], r_ref[...]) + got_ref[rows, :].astype(F32)).astype(BF16)
        for b in range(4):
            row = i * 4 + b
            for q in range(4):
                part = total[b * T : (b + 1) * T, q * 128 : (q + 1) * 128]
                first, second = sides(part[:H], part[H:])
                y_ref[row * 8 + 2 * q] = first
                y_ref[row * 8 + 2 * q + 1] = second
        return carry

    lax.fori_loop(0, 4, body, 0)


def incoming_kernel(x_ref, l_ref, r_ref):
    def gather(c, carry):
        at = pl.multiple_of(c * T, T)
        for q in range(8):
            low, high = sides(x_ref[16 * q + c], x_ref[16 * q + 8 + c])
            cols = slice(q * 128, (q + 1) * 128)
            l_ref[pl.ds(at, H), cols] = low[:H]
            l_ref[pl.ds(at + H, H), cols] = high[:H]
            r_ref[pl.ds(at, H), cols] = low[H:]
            r_ref[pl.ds(at + H, H), cols] = high[H:]
        return carry

    lax.fori_loop(0, 8, gather, 0)


def incoming_sum_kernel(l_ref, r_ref, got_ref, y_ref):
    core = lax.axis_index("core")

    def body(i, carry):
        right = r_ref[pl.ds(pl.multiple_of(i * 128, 128), 128), :]
        for left_ref, parity in ((l_ref, core), (got_ref, 1 - core)):
            total = nt_dot(right, left_ref[...]).astype(BF16)
            for b in range(2):
                c = i * 2 + b
                for q in range(4):
                    part = total[b * T : (b + 1) * T, q * 128 : (q + 1) * 128]
                    first, second = sides(part[:H], part[H:])
                    y_ref[(4 * q + parity) * 8 + c] = first
                    y_ref[(4 * q + 2 + parity) * 8 + c] = second
        return carry

    lax.fori_loop(0, 4, body, 0)


def call(kernel, outs, scratch=(), flops=0, moved=0):
    return pl.pallas_call(
        kernel,
        out_shape=[jax.ShapeDtypeStruct(s, d) for s, d in outs],
        scratch_shapes=[pltpu.VMEM(s, d) for s, d in scratch],
        compiler_params=pltpu.CompilerParams(vmem_limit_bytes=VMEM_LIMIT),
        cost_estimate=pl.CostEstimate(flops=flops, bytes_accessed=moved, transcendentals=0),
    )


CHIPS = ("row", "col", "yh")
SWAP = ((0, 1), (1, 0))


def exchange(x):
    return lax.all_to_all(x, CHIPS, split_axis=0, concat_axis=0, tiled=True)


def on_device(
    pair, token_mask, in_gain, in_bias, proj_weight, gate_weight, mid_gain, mid_bias, out_weight
):
    row = lax.axis_index("row")
    block = lax.axis_index("col") * 4 + lax.axis_index("yh") * 2 + lax.axis_index("core")
    row_mask = lax.dynamic_slice_in_dim(token_mask, row * T, T).astype(F32)
    col_mask = lax.dynamic_slice_in_dim(token_mask, block * T, T).astype(F32)
    mask0 = (row_mask.reshape(2, H).T[:, :, None] * col_mask).reshape(H, 2 * T)
    mask1 = (col_mask.reshape(2, H).T[:, :, None] * row_mask).reshape(H, 2 * T)
    gates = ((H, 2 * T, C), F32)
    wide = ((C, T, 2 * T), BF16)
    narrow = ((C, H, 2 * T), BF16)
    line = ((C, BLK, 2 * T), F32)

    x, gate0 = call(first_kernel, [wide, gates], [line, line])(
        pair, mask0, in_gain[:1], in_bias[:1], proj_weight[0], gate_weight[0]
    )
    x = exchange(x)
    left, right, other = call(
        outgoing_kernel,
        [((1024, 512), BF16), ((512, 512), BF16), ((1024, 512), BF16)],
        [((1024, 512), BF16)],
    )(x)
    got = lax.ppermute(other, "core", SWAP)
    (y,) = call(outgoing_sum_kernel, [narrow])(left, right, got)
    y = exchange(y)
    x, gate1, current = call(middle_kernel, [wide, gates, ((T, T, C), F32)], [line, line])(
        y, pair, gate0, mid_gain[0][:, None], mid_bias[0][:, None], out_weight[0],
        mask1, in_gain[1:], in_bias[1:], proj_weight[1], gate_weight[1],
    )
    x = exchange(x)
    left, right = call(incoming_kernel, [((512, 1024), BF16), ((512, 1024), BF16)])(x)
    got = lax.ppermute(left, "core", SWAP)
    (y,) = call(incoming_sum_kernel, [narrow])(left, right, got)
    y = exchange(y)
    (out,) = call(last_kernel, [((T, T, C), F32)], [line])(
        y, current, gate1, mid_gain[1][:, None], mid_bias[1][:, None], out_weight[1]
    )
    return out


def solution(mesh):
    inner = jax.sharding.Mesh(mesh.devices.reshape(16, 4, 2, 2), ("row", "col", "yh", "core"))
    spec = P("row", ("col", "yh", "core"), None)
    return jax.shard_map(
        on_device,
        mesh=inner,
        in_specs=(spec, P(), P(), P(), P(), P(), P(), P(), P()),
        out_specs=spec,
        check_vma=False,
    )
```

time: 1160 us -> 250 us (0.22); the launches traced: 1140 us -> 249 us
  waiting for transfers between devices: 717 us -> 65.2 us
  local copies, waits for them, and re-layouts: 173 us -> 12.1 us
  blocking collectives: 171 us -> 126 us
  matrix products: 38.1 us -> 0 us
  Pallas kernels: 0 us -> 31.4 us
  other arithmetic: 15.1 us -> 0.84 us
  between operations: 13.9 us -> 0.14 us
    all_gather x3 -> x0, waiting for transfers between devices: 505 us -> none  [the longest x1 295 us: outgoing(): lax.all_gather(right_block, 'row', axis=1, tiled=True)]
    all_to_all x3 -> x2, waiting for transfers between devices: 160 us -> 59.9 us  [exchange(): return lax.all_to_all(x, CHIPS, split_axis=0, concat_axis=0, tiled=True)]
    all_to_all x12 -> x0, local copies, waits for them, and re-layouts: 66.4 us -> none  [the longest x2 23.9 us: incoming(): lax.all_to_all(all_left, 'row', split_axis=2, concat_axis=1, tiled=True)]
    unnamed x38 -> x20, local copies, waits for them, and re-layouts: 69.4 us -> 7.43 us
    psum x4 -> x0, blocking collectives: 60.5 us -> none  [the longest x2 33.6 us: on_device(): lax.psum(jnp.sum(triangle, axis=0).astype(jnp.bfloat16), 'ch')]
    reduce_scatter x1 -> x0, waiting for transfers between devices: 51.8 us -> none  [outgoing(): lax.psum_scatter(partial_sums.astype(jnp.bfloat16), 'col', scatter_dimens...]
    dot_general x8 -> x0, matrix products: 38.1 us -> none  [the longest x2 10.9 us: on_device(): jnp.einsum('cij,cd->ijd', normed_mid, out_weight[section], preferred_elem...]
    pallas_call x0 -> x7, Pallas kernels: none -> 31.4 us  [the longest x1 8.91 us: on_device(): call(middle_kernel, [wide, gates, ((T, T, C), F32)], [line, line])]
  transfers between devices with their start and end apart: 7 -> 4, of which waited for: 7 -> 4; matrix products, arithmetic and copies ran while one was open for 7% -> 1% of each run, Pallas kernels for 0% -> 0%
where the time goes in v1:
time: 250 us; the launch traced here: 249 us
  blocking collectives  126 us (50%)
  waiting for transfers between devices  65.2 us (26%)
  Pallas kernels  31.4 us (13%)
  starting transfers between devices  13.3 us (5%)
  local copies, waits for them, and re-layouts  12.1 us (5%)
    all_to_all x2, blocking collectives, exchange(): return lax.all_to_all(x, CHIPS, split_axis=0, concat_axis=0, tiled=True)  126 us
    all_to_all x2, waiting for transfers between devices, exchange(): return lax.all_to_all(x, CHIPS, split_axis=0, concat_axis=0, tiled=True)  59.9 us
    all_to_all x2, starting transfers between devices, exchange(): return lax.all_to_all(x, CHIPS, split_axis=0, concat_axis=0, tiled=True)  13.1 us
    pallas_call x1, Pallas kernels, on_device(): call(middle_kernel, [wide, gates, ((T, T, C), F32)], [line, line])  8.91 us
    unnamed x20, local copies, waits for them, and re-layouts  7.43 us
    pallas_call x1, Pallas kernels, on_device(): call(last_kernel, [((T, T, C), F32)], [line])  5.77 us
    pallas_call x1, Pallas kernels, on_device(): call(first_kernel, [wide, gates], [line, line])  5.34 us
  transfers between devices with their start and end apart: 4, of which 4 were waited for; matrix products, arithmetic and copies ran while one was open for 1% of the time, Pallas kernels for 0%

profile of v1, /device:TPU:32, one launch (start us, length us, event | category | flops | bytes accessed | tf_op | source)
XLA Modules:
  0.0 249.1 jit_solution(15741684987124876798)
XLA Ops:
  0.0 0.8 dynamic-slice_convert_fusion
  1.3 1.0 slice_bitcast_fusion
  2.3 0.8 slice_bitcast_fusion.3
  3.1 0.8 fusion
  3.8 1.6 copy-done
  5.4 5.3 %shard_map.91 = (bf16[128,64,128]{2,1,0:T(8,128)(2,1)S(1)}, f32[32,128,128]{2,1,0:T(8,128)S(1)}) custom-call(f32[64,64,128]{2,1,0:T(8,128)S(1)} %copy-done, f32[32,128]{1,0:T(8,128)S(1)} %broadcast_multiply_fusion.1.mask_ref, f32[1,128]{1,0:T(1,128)S(1)} %get-tuple-element.41.gain_ref, f32[1,128]{1,0:T(1,128)S(1)} %get-tuple-element.38.bias_ref, ...), custom_call_target="tpu_custom_call" | custom-call | tf_op jit(solution)/shard_map/pallas_call | solution.py:229
  10.8 1.3 copy-done.6
  12.1 67.7 %all_to_all.20.x_ref = bf16[128,64,128]{2,1,0:T(8,128)(2,1)S(1)} all-to-all(bf16[128,64,128]{2,1,0:T(8,128)(2,1)S(1)} %get-tuple-element.15), channel_id=1, replica_groups=mesh['row'=16,'col'=4,'yh'=2,'core'=2] {'row','col','yh'}, dimensions={0} | all-to-all | bytes 4194304 | tf_op jit(solution)/shard_map/all_to_all | solution.py:212
  79.8 3.1 %shard_map.92 = (bf16[1024,512]{1,0:T(8,128)(2,1)S(1)}, bf16[512,512]{1,0:T(8,128)(2,1)S(1)}, bf16[1024,512]{1,0:T(8,128)(2,1)S(1)}) custom-call(bf16[128,64,128]{2,1,0:T(8,128)(2,1)S(1)} %all_to_all.20.x_ref), custom_call_target="tpu_custom_call" | custom-call | tf_op jit(solution)/shard_map/pallas_call | solution.py:233
  82.9 0.1 collective-permute-start
  83.0 2.6 %collective-permute-done.got_ref = bf16[1024,512]{1,0:T(8,128)(2,1)S(1)} collective-permute-done((bf16[1024,512]{1,0:T(8,128)(2,1)S(1)}, bf16[1024,512]{1,0:T(8,128)(2,1)S(1)}, u32[]{:S(2)}, u32[]{:S(2)}) %collective-permute-start) | collective-permute-done | bytes 1048608 | tf_op jit(solution)/shard_map/ppermute | solution.py:238
  85.6 2.7 %shard_map.93 = bf16[128,32,128]{2,1,0:T(8,128)(2,1)} custom-call(bf16[1024,512]{1,0:T(8,128)(2,1)S(1)} %get-tuple-element.16.l_ref, bf16[512,512]{1,0:T(8,128)(2,1)S(1)} %get-tuple-element.17.r_ref, bf16[1024,512]{1,0:T(8,128)(2,1)S(1)} %collective-permute-done.got_ref), custom_call_target="tpu_custom_call" | custom-call | tf_op jit(solution)/shard_map/pallas_call | solution.py:239
  88.3 6.6 %all-to-all-start.1 = ((bf16[128,32,128]{2,1,0:T(8,128)(2,1)}), bf16[128,32,128]{2,1,0:T(8,128)(2,1)S(1)}, u32[]{:S(2)}, u32[]{:S(2)}) async-start(bf16[128,32,128]{2,1,0:T(8,128)(2,1)} %shard_map.93), calls=%async_computation.1 | async-start | bytes 2097152 | tf_op jit(solution)/shard_map/all_to_all | solution.py:212
  94.9 0.1 copy.11
  95.3 0.1 copy.12.mgain_ref
  95.4 0.1 copy.13.mbias_ref
  95.6 0.8 slice_bitcast_fusion.2
  96.3 29.3 %all-to-all-done.1.y_ref = bf16[128,32,128]{2,1,0:T(8,128)(2,1)S(1)} async-done(((bf16[128,32,128]{2,1,0:T(8,128)(2,1)}), bf16[128,32,128]{2,1,0:T(8,128)(2,1)S(1)}, u32[]{:S(2)}, u32[]{:S(2)}) %all-to-all-start.1) | async-done | bytes 1048608 | tf_op jit(solution)/shard_map/all_to_all | solution.py:212
  125.7 1.6 copy-done.7
  127.3 8.9 %shard_map.94 = (bf16[128,64,128]{2,1,0:T(8,128)(2,1)S(1)}, f32[32,128,128]{2,1,0:T(8,128)S(1)}, f32[64,64,128]{2,1,0:T(8,128)S(1)}) custom-call(bf16[128,32,128]{2,1,0:T(8,128)(2,1)S(1)} %all-to-all-done.1.y_ref, f32[64,64,128]{2,1,0:T(8,128)S(1)} %copy-done.1, f32[32,128,128]{2,1,0:T(8,128)S(1)} %copy-done.7, f32[128,1]{1,0:T(8,128)S(1)} %copy.12.mgain_ref, ...), custom_call_target="tpu_custom_call" | custom-call | tf_op jit(solution)/shard_map/pallas_call | solution.py:241
  136.2 1.3 copy-done.2
  137.5 58.4 %all_to_all.21.x_ref = bf16[128,64,128]{2,1,0:T(8,128)(2,1)S(1)} all-to-all(bf16[128,64,128]{2,1,0:T(8,128)(2,1)S(1)} %get-tuple-element.20), channel_id=1, replica_groups=mesh['row'=16,'col'=4,'yh'=2,'core'=2] {'row','col','yh'}, dimensions={0} | all-to-all | bytes 4194304 | tf_op jit(solution)/shard_map/all_to_all | solution.py:212
  195.9 1.2 shard_map.95
  197.1 0.1 collective-permute-start.1
  197.2 2.6 %collective-permute-done.1.got_ref = bf16[512,1024]{1,0:T(8,128)(2,1)S(1)} collective-permute-done((bf16[512,1024]{1,0:T(8,128)(2,1)S(1)}, bf16[512,1024]{1,0:T(8,128)(2,1)S(1)}, u32[]{:S(2)}, u32[]{:S(2)}) %collective-permute-start.1) | collective-permute-done | bytes 1048608 | tf_op jit(solution)/shard_map/ppermute | solution.py:247
  199.8 4.6 %shard_map.96 = bf16[128,32,128]{2,1,0:T(8,128)(2,1)} custom-call(bf16[512,1024]{1,0:T(8,128)(2,1)S(1)} %get-tuple-element.21.l_ref, bf16[512,1024]{1,0:T(8,128)(2,1)S(1)} %get-tuple-element.22.r_ref, bf16[512,1024]{1,0:T(8,128)(2,1)S(1)} %collective-permute-done.1.got_ref), custom_call_target="tpu_custom_call" | custom-call | tf_op jit(solution)/shard_map/pallas_call | solution.py:248
  204.4 6.6 %all-to-all-start.3 = ((bf16[128,32,128]{2,1,0:T(8,128)(2,1)}), bf16[128,32,128]{2,1,0:T(8,128)(2,1)S(1)}, u32[]{:S(2)}, u32[]{:S(2)}) async-start(bf16[128,32,128]{2,1,0:T(8,128)(2,1)} %shard_map.96), calls=%async_computation.3 | async-start | bytes 2097152 | tf_op jit(solution)/shard_map/all_to_all | solution.py:212
  210.9 0.1 copy.14.mgain_ref
  211.0 0.1 copy.15.mbias_ref
  211.1 30.6 %all-to-all-done.3.y_ref = bf16[128,32,128]{2,1,0:T(8,128)(2,1)S(1)} async-done(((bf16[128,32,128]{2,1,0:T(8,128)(2,1)}), bf16[128,32,128]{2,1,0:T(8,128)(2,1)S(1)}, u32[]{:S(2)}, u32[]{:S(2)}) %all-to-all-start.3) | async-done | bytes 1048608 | tf_op jit(solution)/shard_map/all_to_all | solution.py:212
  241.8 1.6 copy-done.5
  243.3 5.8 %shard_map.97 = f32[64,64,128]{2,1,0:T(8,128)} custom-call(bf16[128,32,128]{2,1,0:T(8,128)(2,1)S(1)} %all-to-all-done.3.y_ref, f32[64,64,128]{2,1,0:T(8,128)S(1)} %copy-done.5, f32[32,128,128]{2,1,0:T(8,128)S(1)} %copy-done.3, f32[128,1]{1,0:T(8,128)S(1)} %copy.14.mgain_ref, f32[128,1]{1,0:T(8,128)S(1)} %copy.15.mbias_ref, ...), custom_call_target="tpu_custom_call" | custom-call | tf_op jit(solution)/shard_map/pallas_call | solution.py:250
  (30 shorter events, 0.8 us)
Async XLA Ops:
  3.8 1.6 copy-start
  10.8 1.3 copy-start.6
  82.9 2.7 %collective-permute-start = (bf16[1024,512]{1,0:T(8,128)(2,1)S(1)}, bf16[1024,512]{1,0:T(8,128)(2,1)S(1)}, u32[]{:S(2)}, u32[]{:S(2)}) collective-permute-start(bf16[1024,512]{1,0:T(8,128)(2,1)S(1)} %get-tuple-element.18), channel_id=1, source_target_pairs={{0,1},{1,0},{2,3},{3,2},{4,5},{5,4},{6,7},{7,6},{8,9},{9,8},{10,11... | collective-permute-start | bytes 3145736 | tf_op jit(solution)/shard_map/ppermute | solution.py:238
  85.6 9.7 %copy-start.8 = (f32[2,128]{1,0:T(2,128)S(1)}, f32[2,128]{1,0:T(2,128)}, u32[]{:S(2)}) copy-start(f32[2,128]{1,0:T(2,128)} %param.15) | copy-start | bytes 3076
  85.6 9.8 %copy-start.9 = (f32[2,128]{1,0:T(2,128)S(1)}, f32[2,128]{1,0:T(2,128)}, u32[]{:S(2)}) copy-start(f32[2,128]{1,0:T(2,128)} %param.16) | copy-start | bytes 3076
  88.3 37.4 %copy-start.1 = (f32[64,64,128]{2,1,0:T(8,128)S(1)}, f32[64,64,128]{2,1,0:T(8,128)}, u32[]{:S(2)}) copy-start(f32[64,64,128]{2,1,0:T(8,128)} %z_ref.3) | copy-start | bytes 6291460
  88.3 37.4 %all-to-all-start.1 = ((bf16[128,32,128]{2,1,0:T(8,128)(2,1)}), bf16[128,32,128]{2,1,0:T(8,128)(2,1)S(1)}, u32[]{:S(2)}, u32[]{:S(2)}) async-start(bf16[128,32,128]{2,1,0:T(8,128)(2,1)} %shard_map.93), calls=%async_computation.1 | async-start | bytes 2097152 | tf_op jit(solution)/shard_map/all_to_all | solution.py:212
  125.7 1.6 copy-start.7
  136.2 1.3 copy-start.2
  137.5 58.4 %copy-start.4 = (f32[64,64,128]{2,1,0:T(8,128)}, f32[64,64,128]{2,1,0:T(8,128)S(1)}, u32[]{:S(2)}) copy-start(f32[64,64,128]{2,1,0:T(8,128)S(1)} %get-tuple-element.23.z_ref) | copy-start | bytes 6291460
  197.1 2.7 %collective-permute-start.1 = (bf16[512,1024]{1,0:T(8,128)(2,1)S(1)}, bf16[512,1024]{1,0:T(8,128)(2,1)S(1)}, u32[]{:S(2)}, u32[]{:S(2)}) collective-permute-start(bf16[512,1024]{1,0:T(8,128)(2,1)S(1)} %get-tuple-element.21.l_ref), channel_id=1, source_target_pairs={{0,1},{1,0},{2,3},{3,2},{4,5},{5,4},{6,7},{7,6},{8,9},{9,8},{10,11... | collective-permute-start | bytes 3145736 | tf_op jit(solution)/shard_map/ppermute | solution.py:247
  204.4 37.4 %copy-start.3 = (f32[32,128,128]{2,1,0:T(8,128)S(1)}, f32[32,128,128]{2,1,0:T(8,128)}, u32[]{:S(2)}) copy-start(f32[32,128,128]{2,1,0:T(8,128)} %copy-done.2) | copy-start | bytes 6291460
  204.4 37.4 %all-to-all-start.3 = ((bf16[128,32,128]{2,1,0:T(8,128)(2,1)}), bf16[128,32,128]{2,1,0:T(8,128)(2,1)S(1)}, u32[]{:S(2)}, u32[]{:S(2)}) async-start(bf16[128,32,128]{2,1,0:T(8,128)(2,1)} %shard_map.96), calls=%async_computation.3 | async-start | bytes 2097152 | tf_op jit(solution)/shard_map/all_to_all | solution.py:212
  241.8 1.6 copy-start.5

commit v2 on v1

v2 whole, which is shorter than its diff:
```python
import jax
import jax.numpy as jnp
from jax import lax
from jax.experimental import pallas as pl
from jax.experimental.pallas import tpu as pltpu
from jax.sharding import PartitionSpec as P

F32 = jnp.float32
BF16 = jnp.bfloat16
C = 128
T = 64
H = 32
BLK = 16
VMEM_LIMIT = 24 * 1024 * 1024
FIRST_LIMIT = 56 * 1024 * 1024


def sigmoid(x):
    return 0.5 * jnp.tanh(0.5 * x) + 0.5


def layer_norm(values, gain, bias):
    average = jnp.mean(values, axis=-1, keepdims=True)
    centred = values - average
    spread = jnp.mean(centred * centred, axis=-1, keepdims=True)
    return centred * lax.rsqrt(spread + 1e-05) * gain + bias


def lanes_twice(mask_ref, block):
    chunk = mask_ref[:, pl.ds(pl.multiple_of(lax.div(block, 2) * 2 * T, 2 * T), 2 * T)].astype(F32)
    turned = jnp.concatenate([chunk[:, T:], chunk[:, :T]], axis=1)
    lane = lax.broadcasted_iota(jnp.int32, (1, 2 * T), 1)
    keep = lax.div(lane, T) == lax.rem(block, 2)
    return jnp.where(keep, chunk, turned)


def line_mask(token_ref, start, s, across):
    lane = lax.broadcasted_iota(jnp.int32, (1, 2 * T), 1)
    first, second = token_ref[start + s].astype(F32), token_ref[start + s + H].astype(F32)
    return jnp.where(lane < T, first, second) * across


def row_block():
    return lax.axis_index("z") * 2 + lax.axis_index("yl")


def col_block():
    return lax.axis_index("x") * 4 + lax.axis_index("yh") * 2 + lax.axis_index("core")


def column(row):
    shape = (C, C)
    eye = lax.broadcasted_iota(jnp.int32, shape, 0) == lax.broadcasted_iota(jnp.int32, shape, 1)
    return jnp.sum(jnp.where(eye, jnp.broadcast_to(row, shape), 0.0), axis=1, keepdims=True)


def project_block(load, block, mask, gain, bias, w, g, x_ref, gate_ref, sl_ref, sr_ref):
    for t in range(0, BLK, 2):
        s = block * BLK + t
        lines = jnp.concatenate([load(s), load(s + H), load(s + 1), load(s + 1 + H)], axis=0)
        normed = layer_norm(lines, gain, bias).astype(BF16)
        p = lax.dot_general(
            w, normed, (((0,), (1,)), ((), ())), preferred_element_type=F32
        )
        gate = sigmoid(jnp.dot(normed, g, preferred_element_type=F32))
        gate_ref[s] = gate[:C]
        gate_ref[s + 1] = gate[C:]
        left = sigmoid(p[:C]) * p[C : 2 * C]
        right = sigmoid(p[2 * C : 3 * C]) * p[3 * C :]
        for u in range(2):
            keep = mask(s + u)
            sl_ref[:, t + u, :] = left[:, u * C : (u + 1) * C] * keep
            sr_ref[:, t + u, :] = right[:, u * C : (u + 1) * C] * keep
    x_ref[:, pl.ds(pl.multiple_of(block * BLK, BLK), BLK), :] = sl_ref[...].astype(BF16)
    x_ref[:, pl.ds(pl.multiple_of(H + block * BLK, BLK), BLK), :] = sr_ref[...].astype(BF16)


def first_kernel(
    z_hbm, token_hbm, mask_hbm, gain_hbm, bias_hbm, w_hbm, g_hbm, x_hbm, gate_hbm, sl_ref, sr_ref,
    z_ref, token_ref, mask_ref, gain_ref, bias_ref, w_ref, g_ref, x_ref, gate_ref, small_sem, z_sem, out_sem,
):
    small = [
        pltpu.make_async_copy(source, to, small_sem.at[n])
        for n, (source, to) in enumerate(
            (
                (gain_hbm, gain_ref), (bias_hbm, bias_ref), (mask_hbm, mask_ref), (token_hbm, token_ref),
                (w_hbm.at[0], w_ref), (g_hbm.at[0], g_ref),
            )
        )
    ]
    parts = []
    for block in range(H // BLK):
        for half in range(2):
            lines = pl.ds(half * H + block * BLK, BLK)
            parts.append(pltpu.make_async_copy(z_hbm.at[lines], z_ref.at[lines], z_sem.at[len(parts)]))
    for copy in small + parts:
        copy.start()
    for copy in small:
        copy.wait()
    gain, bias = gain_ref[0:1], bias_ref[0:1]
    across = lanes_twice(mask_ref, col_block())
    start = row_block() * T
    copies = []
    for block in range(H // BLK):
        parts[2 * block].wait()
        parts[2 * block + 1].wait()
        project_block(
            lambda s: z_ref[s], block, lambda s: line_mask(token_ref, start, s, across), gain, bias,
            w_ref[...], g_ref[...], x_ref, gate_ref, sl_ref, sr_ref,
        )
        for half in range(2):
            lines = pl.ds(half * H + block * BLK, BLK)
            copies.append(
                pltpu.make_async_copy(x_ref.at[:, lines], x_hbm.at[:, lines], out_sem.at[len(copies)])
            )
            copies[-1].start()
        lines = pl.ds(block * BLK, BLK)
        copies.append(pltpu.make_async_copy(gate_ref.at[lines], gate_hbm.at[lines], out_sem.at[len(copies)]))
        copies[-1].start()
    for copy in copies:
        copy.wait()


def update_block(block, y_ref, gain, bias, ow, gate_ref, s_ref, emit):
    y = y_ref[:, pl.ds(pl.multiple_of(block * BLK, BLK), BLK), :].astype(F32)
    average = jnp.sum(y, axis=0) * (1.0 / C)
    centred = y - average[None]
    spread = jnp.sum(centred * centred, axis=0) * (1.0 / C)
    s_ref[...] = centred * lax.rsqrt(spread + 1e-05)[None]
    for t in range(BLK):
        s = block * BLK + t
        normed = (s_ref[:, t, :] * gain + bias).astype(BF16)
        update = lax.dot_general(
            normed, ow, (((0,), (0,)), ((), ())), preferred_element_type=F32
        )
        emit(s, gate_ref[s] * update)


def middle_kernel(
    y_ref, z_ref, gate0_ref, mgain_ref, mbias_ref, ow_ref, token_ref, mask_ref, gain_ref, bias_ref,
    w_ref, g_ref, x_ref, gate_ref, zn_ref, sl_ref, sr_ref,
):
    mgain, mbias = column(mgain_ref[0:1]), column(mbias_ref[0:1])
    gain, bias = gain_ref[1:2], bias_ref[1:2]
    across = lanes_twice(mask_ref, row_block())
    start = col_block() * T

    def emit(s, change):
        zn_ref[s] = z_ref[s] + change[:T]
        zn_ref[s + H] = z_ref[s + H] + change[T:]

    def body(block, carry):
        update_block(block, y_ref, mgain, mbias, ow_ref[0], gate0_ref, sl_ref, emit)
        return carry

    lax.fori_loop(0, H // BLK, body, 0)

    for block in range(H // BLK):
        project_block(
            lambda s: zn_ref[:, s, :], block, lambda s: line_mask(token_ref, start, s, across), gain, bias,
            w_ref[1], g_ref[1], x_ref, gate_ref, sl_ref, sr_ref,
        )


def last_kernel(y_ref, z_ref, gate_ref, mgain_ref, mbias_ref, ow_ref, out_ref, s_ref):
    mgain, mbias = column(mgain_ref[1:2]), column(mbias_ref[1:2])

    def emit(s, change):
        out_ref[:, s, :] = z_ref[:, s, :] + change[:T]
        out_ref[:, s + H, :] = z_ref[:, s + H, :] + change[T:]

    for block in range(H // BLK):
        update_block(block, y_ref, mgain, mbias, ow_ref[1], gate_ref, s_ref, emit)


def sides(x0, x1):
    low = jnp.concatenate([x0[:, :T], x1[:, :T]], axis=1)
    high = jnp.concatenate([x0[:, T:], x1[:, T:]], axis=1)
    return low, high


def nt_dot(a, b):
    return lax.dot_general(a, b, (((1,), (1,)), ((), ())), preferred_element_type=F32)


def chip(row, col):
    return lax.div(row, 2) * 16 + lax.rem(col, 2) * 8 + lax.rem(row, 2) * 4 + lax.div(col, 2)


def outgoing_kernel(x_ref, l_ref, r_ref, other_ref, rs_ref):
    core = lax.axis_index("core")

    def gather(row, carry):
        at = pl.multiple_of(row * T, T)
        to = pl.multiple_of(lax.rem(row, 2) * 512 + lax.div(row, 2) * T, T)
        base = chip(row, 0)
        for q in range(4):
            low, high = sides(x_ref[base + q], x_ref[base + 8 + q])
            cols = slice(q * 128, (q + 1) * 128)
            l_ref[pl.ds(at, H), cols] = low[:H]
            l_ref[pl.ds(at + H, H), cols] = high[:H]
            rs_ref[pl.ds(to, H), cols] = low[H:]
            rs_ref[pl.ds(to + H, H), cols] = high[H:]
        return carry

    lax.fori_loop(0, 16, gather, 0)
    r_ref[...] = rs_ref[pl.ds(pl.multiple_of(core * 512, 512), 512), :]
    send = rs_ref[pl.ds(pl.multiple_of((1 - core) * 512, 512), 512), :]

    def multiply(i, carry):
        rows = pl.ds(pl.multiple_of(i * 256, 256), 256)
        other_ref[rows, :] = nt_dot(l_ref[rows, :], send).astype(BF16)
        return carry

    lax.fori_loop(0, 4, multiply, 0)


def outgoing_sum_kernel(l_ref, r_ref, got_ref, y_ref):
    def body(i, carry):
        rows = pl.ds(pl.multiple_of(i * 256, 256), 256)
        total = (nt_dot(l_ref[rows, :], r_ref[...]) + got_ref[rows, :].astype(F32)).astype(BF16)
        for b in range(4):
            base = chip(i * 4 + b, 0)
            for q in range(4):
                part = total[b * T : (b + 1) * T, q * 128 : (q + 1) * 128]
                first, second = sides(part[:H], part[H:])
                y_ref[base + q] = first
                y_ref[base + 8 + q] = second
        return carry

    lax.fori_loop(0, 4, body, 0)


def incoming_kernel(x_ref, l_ref, r_ref):
    def gather(c, carry):
        at = pl.multiple_of(c * T, T)
        base = chip(0, c)
        for q in range(8):
            low, high = sides(x_ref[16 * q + base], x_ref[16 * q + 4 + base])
            cols = slice(q * 128, (q + 1) * 128)
            l_ref[pl.ds(at, H), cols] = low[:H]
            l_ref[pl.ds(at + H, H), cols] = high[:H]
            r_ref[pl.ds(at, H), cols] = low[H:]
            r_ref[pl.ds(at + H, H), cols] = high[H:]
        return carry

    lax.fori_loop(0, 8, gather, 0)


def incoming_half(l_ref, r_ref, write):
    def body(i, carry):
        right = r_ref[pl.ds(pl.multiple_of(i * 128, 128), 128), :]
        total = nt_dot(right, l_ref[...]).astype(BF16)
        for b in range(2):
            base = chip(0, i * 2 + b)
            for q in range(4):
                part = total[b * T : (b + 1) * T, q * 128 : (q + 1) * 128]
                first, second = sides(part[:H], part[H:])
                write(2 * q, base, first)
                write(2 * q + 1, base, second)
        return carry

    lax.fori_loop(0, 4, body, 0)


def incoming_own_kernel(l_ref, r_ref, half_ref):
    def write(plane, base, value):
        half_ref[plane * 16 + base] = value

    incoming_half(l_ref, r_ref, write)


def incoming_sum_kernel(l_ref, r_ref, half_ref, y_ref):
    own = lax.axis_index("core")

    def write(plane, base, value):
        y_ref[plane * 16 + (1 - own) * 4 + base] = value

    incoming_half(l_ref, r_ref, write)
    for plane in range(8):
        for y in range(2):
            y_ref[pl.ds(plane * 16 + y * 8 + own * 4, 4)] = half_ref[pl.ds(plane * 16 + y * 8, 4)]


def call(kernel, outs, scratch=(), specs=None, out_specs=None, limit=VMEM_LIMIT):
    return pl.pallas_call(
        kernel,
        out_shape=[jax.ShapeDtypeStruct(s, d) for s, d in outs],
        scratch_shapes=[pltpu.VMEM(*m) if isinstance(m, tuple) else m for m in scratch],
        compiler_params=pltpu.CompilerParams(vmem_limit_bytes=limit),
        **({} if specs is None else {"in_specs": specs}),
        **({} if out_specs is None else {"out_specs": out_specs}),
    )


VMEM_SPEC = pl.BlockSpec(memory_space=pltpu.VMEM)
SMEM_SPEC = pl.BlockSpec(memory_space=pltpu.SMEM)
HBM_SPEC = pl.BlockSpec(memory_space=pltpu.HBM)
CHIPS = ("z", "yh", "yl", "x")
SWAP = ((0, 1), (1, 0))


def exchange(x):
    return lax.all_to_all(x, CHIPS, split_axis=0, concat_axis=0, tiled=True)


def on_device(
    pair, token_mask, in_gain, in_bias, proj_weight, gate_weight, mid_gain, mid_bias, out_weight
):
    mask = token_mask[None]
    gates = ((H, 2 * T, C), F32)
    wide = ((C, T, 2 * T), BF16)
    narrow = ((C, H, 2 * T), BF16)
    line = ((C, BLK, 2 * T), F32)

    x, gate0 = call(
        first_kernel,
        [wide, gates],
        [
            line, line, ((T, T, C), F32), pltpu.SMEM((1024,), jnp.int32), ((1, 1024), jnp.int32), ((2, C), F32),
            ((2, C), F32), ((C, 4 * C), BF16), ((C, C), BF16), wide, gates, pltpu.SemaphoreType.DMA((6,)),
            pltpu.SemaphoreType.DMA((4,)), pltpu.SemaphoreType.DMA((6,)),
        ],
        [HBM_SPEC] * 7,
        [HBM_SPEC] * 2,
        FIRST_LIMIT,
    )(
        pair, token_mask, mask, in_gain, in_bias, proj_weight, gate_weight
    )
    x = exchange(x)
    left, right, other = call(
        outgoing_kernel,
        [((1024, 512), BF16), ((512, 512), BF16), ((1024, 512), BF16)],
        [((1024, 512), BF16)],
    )(x)
    got = lax.ppermute(other, "core", SWAP)
    (y,) = call(outgoing_sum_kernel, [narrow])(left, right, got)
    y = exchange(y)
    x, gate1, current = call(middle_kernel, [wide, gates, ((T, T, C), F32)], [line, line], [VMEM_SPEC] * 6 + [SMEM_SPEC] + [VMEM_SPEC] * 5)(
        y, pair, gate0, mid_gain, mid_bias, out_weight,
        token_mask, mask, in_gain, in_bias, proj_weight, gate_weight,
    )
    x = exchange(x)
    left, right = call(incoming_kernel, [((512, 1024), BF16), ((512, 1024), BF16)])(x)
    got = lax.ppermute(left, "core", SWAP)
    (half,) = call(incoming_own_kernel, [narrow])(left, right)
    (y,) = call(incoming_sum_kernel, [narrow])(got, right, half)
    y = exchange(y)
    (out,) = call(last_kernel, [((T, T, C), F32)], [line])(
        y, current, gate1, mid_gain, mid_bias, out_weight
    )
    return out


def solution(mesh):
    inner = jax.sharding.Mesh(mesh.devices.reshape(8, 2, 4, 2, 2), ("z", "yl", "x", "yh", "core"))
    spec = P(("z", "yl"), ("x", "yh", "core"), None)
    return jax.shard_map(
        on_device,
        mesh=inner,
        in_specs=(spec, P(), P(), P(), P(), P(), P(), P(), P()),
        out_specs=spec,
        check_vma=False,
    )
```

time: 250 us -> 240 us (0.960)
  blocking collectives: 126 us -> 203 us
  waiting for transfers between devices: 65.2 us -> 3.05 us
  starting transfers between devices: 13.3 us -> 0.19 us
  local copies, waits for them, and re-layouts: 12.1 us -> 0.05 us
    all_to_all x2 -> x4, blocking collectives: 126 us -> 203 us  [exchange(): return lax.all_to_all(x, CHIPS, split_axis=0, concat_axis=0, tiled=True)]
    all_to_all x2 -> x0, waiting for transfers between devices: 59.9 us -> none  [exchange(): return lax.all_to_all(x, CHIPS, split_axis=0, concat_axis=0, tiled=True)]
    all_to_all x2 -> x0, starting transfers between devices: 13.1 us -> none  [exchange(): return lax.all_to_all(x, CHIPS, split_axis=0, concat_axis=0, tiled=True)]
    unnamed x20, local copies, waits for them, and re-layouts: 7.43 us -> 0.05 us
    pallas_call x3 -> x4, Pallas kernels: 18.8 us -> 22.2 us  [the longest x1 9.64 us: on_device(): call(middle_kernel, [wide, gates, ((T, T, C), F32)], [line, line], [VMEM_...]
    squeeze x3 -> x0, local copies, waits for them, and re-layouts: 2.56 us -> none  [the longest x1 0.99 us: on_device(): proj_weight[1]]
  transfers between devices with their start and end apart: 4 -> 2, of which waited for: 4 -> 2; matrix products, arithmetic and copies ran while one was open for 1% -> 0% of each run, Pallas kernels for 0% -> 1%
where the time goes in v2:
time: 240 us
  blocking collectives  203 us (85%)
  Pallas kernels  33.7 us (14%)
  waiting for transfers between devices  3.05 us (1%)
    all_to_all x4, blocking collectives, exchange(): return lax.all_to_all(x, CHIPS, split_axis=0, concat_axis=0, tiled=True)  203 us
    pallas_call x1, Pallas kernels, on_device(): call(middle_kernel, [wide, gates, ((T, T, C), F32)], [line, line], [VMEM_...  9.64 us
    pallas_call x1, Pallas kernels, on_device(): call(first_kernel, [wide, gates], [line, line, ((T, T, C), F32), pltpu.SM...  8.03 us
    pallas_call x1, Pallas kernels, on_device(): call(last_kernel, [((T, T, C), F32)], [line])  5.72 us
  transfers between devices with their start and end apart: 2, of which 2 were waited for; matrix products, arithmetic and copies ran while one was open for 0% of the time, Pallas kernels for 1%

profile of v2, /device:TPU:32, one launch (start us, length us, event | category | flops | bytes accessed | tf_op | source)
XLA Modules:
  0.0 240.0 jit_solution(7991241728311750023)
XLA Ops:
  0.0 8.0 %shard_map.91 = (bf16[128,64,128]{2,1,0:T(8,128)(2,1)}, f32[32,128,128]{2,1,0:T(8,128)}) custom-call(f32[64,64,128]{2,1,0:T(8,128)} %z_ref.1, s32[1024]{0:T(1024)} %token_ref.1, s32[1,1024]{1,0:T(1,128)} %bitcast.1, f32[2,128]{1,0:T(2,128)} %gain_ref.1, f32[2,128]{1,0:T(2,128)} %bias_ref.1, bf16[2,128,512]{2,1,0:T(8,128)(2,1)} %w_ref.1, ...), custom_call_target="tpu_custom_call" | custom-call | tf_op jit(solution)/shard_map/pallas_call | solution.py:316
  8.0 68.5 %all_to_all.20.x_ref = bf16[128,64,128]{2,1,0:T(8,128)(2,1)S(1)} all-to-all(bf16[128,64,128]{2,1,0:T(8,128)(2,1)} %get-tuple-element.15), channel_id=1, replica_groups=mesh['z'=8,'yl'=2,'x'=4,'yh'=2,'core'=2] {'z','yh','yl','x'}, dimensions={0} | all-to-all | bytes 4194304 | tf_op jit(solution)/shard_map/all_to_all | solution.py:304
  76.5 3.1 %shard_map.92 = (bf16[1024,512]{1,0:T(8,128)(2,1)S(1)}, bf16[512,512]{1,0:T(8,128)(2,1)S(1)}, bf16[1024,512]{1,0:T(8,128)(2,1)S(1)}) custom-call(bf16[128,64,128]{2,1,0:T(8,128)(2,1)S(1)} %all_to_all.20.x_ref), custom_call_target="tpu_custom_call" | custom-call | tf_op jit(solution)/shard_map/pallas_call | solution.py:331
  79.6 0.1 collective-permute-start
  79.7 2.6 %collective-permute-done.got_ref = bf16[1024,512]{1,0:T(8,128)(2,1)S(1)} collective-permute-done((bf16[1024,512]{1,0:T(8,128)(2,1)S(1)}, bf16[1024,512]{1,0:T(8,128)(2,1)S(1)}, u32[]{:S(2)}, u32[]{:S(2)}) %collective-permute-start) | collective-permute-done | bytes 1048608 | tf_op jit(solution)/shard_map/ppermute | solution.py:336
  82.3 0.0 copy-start.4
  82.3 0.0 copy-start.5
  82.4 0.0 copy-start.6
  82.4 0.0 copy-start.7
  82.4 0.0 copy-start.8
  82.4 0.0 copy-start.9
  82.4 1.6 shard_map.93
  84.1 37.9 %all_to_all.21.y_ref = bf16[128,32,128]{2,1,0:T(8,128)(2,1)S(1)} all-to-all(bf16[128,32,128]{2,1,0:T(8,128)(2,1)S(1)} %shard_map.93), channel_id=1, replica_groups=mesh['z'=8,'yl'=2,'x'=4,'yh'=2,'core'=2] {'z','yh','yl','x'}, dimensions={0} | all-to-all | bytes 2097152 | tf_op jit(solution)/shard_map/all_to_all | solution.py:304
  121.9 0.0 copy-done
  121.9 0.0 copy-done.1
  121.9 0.0 copy-done.2
  121.9 0.0 copy-done.3
  121.9 0.0 copy-done.4
  121.9 0.0 copy-done.5
  121.9 0.0 copy-done.6
  122.0 0.0 copy-done.7
  122.0 0.0 copy-done.8
  122.0 0.0 copy-done.9
  122.0 9.6 %shard_map.94 = (bf16[128,64,128]{2,1,0:T(8,128)(2,1)S(1)}, f32[32,128,128]{2,1,0:T(8,128)S(1)}, f32[64,64,128]{2,1,0:T(8,128)S(1)}) custom-call(bf16[128,32,128]{2,1,0:T(8,128)(2,1)S(1)} %all_to_all.21.y_ref, f32[64,64,128]{2,1,0:T(8,128)S(1)} %copy-done, f32[32,128,128]{2,1,0:T(8,128)S(1)} %copy-done.1, f32[2,128]{1,0:T(2,128)S(1)} %copy-done.8, ...), custom_call_target="tpu_custom_call" | custom-call | tf_op jit(solution)/shard_map/pallas_call | solution.py:339
  131.6 58.7 %all_to_all.22.x_ref = bf16[128,64,128]{2,1,0:T(8,128)(2,1)S(1)} all-to-all(bf16[128,64,128]{2,1,0:T(8,128)(2,1)S(1)} %get-tuple-element.20), channel_id=1, replica_groups=mesh['z'=8,'yl'=2,'x'=4,'yh'=2,'core'=2] {'z','yh','yl','x'}, dimensions={0} | all-to-all | bytes 4194304 | tf_op jit(solution)/shard_map/all_to_all | solution.py:304
  190.3 1.1 shard_map.95
  191.5 0.1 collective-permute-start.1
  191.6 2.2 shard_map.96.half_ref
  193.8 0.4 collective-permute-done.1.l_ref
  194.2 2.3 shard_map.97
  196.5 37.8 %all_to_all.23.y_ref = bf16[128,32,128]{2,1,0:T(8,128)(2,1)S(1)} all-to-all(bf16[128,32,128]{2,1,0:T(8,128)(2,1)S(1)} %shard_map.97), channel_id=1, replica_groups=mesh['z'=8,'yl'=2,'x'=4,'yh'=2,'core'=2] {'z','yh','yl','x'}, dimensions={0} | all-to-all | bytes 2097152 | tf_op jit(solution)/shard_map/all_to_all | solution.py:304
  234.3 5.7 %shard_map.98 = f32[64,64,128]{2,1,0:T(8,128)} custom-call(bf16[128,32,128]{2,1,0:T(8,128)(2,1)S(1)} %all_to_all.23.y_ref, f32[64,64,128]{2,1,0:T(8,128)S(1)} %get-tuple-element.23.z_ref, f32[32,128,128]{2,1,0:T(8,128)S(1)} %get-tuple-element.24.gate_ref, f32[2,128]{1,0:T(2,128)S(1)} %copy-done.8, f32[2,128]{1,0:T(2,128)S(1)} %copy-done.9, ...), custom_call_target="tpu_custom_call" | custom-call | tf_op jit(solution)/shard_map/pallas_call | solution.py:349
  (4 shorter events, 0.0 us)
Async XLA Ops:
  79.6 2.7 %collective-permute-start = (bf16[1024,512]{1,0:T(8,128)(2,1)S(1)}, bf16[1024,512]{1,0:T(8,128)(2,1)S(1)}, u32[]{:S(2)}, u32[]{:S(2)}) collective-permute-start(bf16[1024,512]{1,0:T(8,128)(2,1)S(1)} %get-tuple-element.18), channel_id=1, source_target_pairs={{0,1},{1,0},{2,3},{3,2},{4,5},{5,4},{6,7},{7,6},{8,9},{9,8},{10,11... | collective-permute-start | bytes 3145736 | tf_op jit(solution)/shard_map/ppermute | solution.py:336
  82.3 39.6 %copy-start = (f32[64,64,128]{2,1,0:T(8,128)S(1)}, f32[64,64,128]{2,1,0:T(8,128)}, u32[]{:S(2)}) copy-start(f32[64,64,128]{2,1,0:T(8,128)} %z_ref.1) | copy-start | bytes 6291460
  82.3 39.6 %copy-start.1 = (f32[32,128,128]{2,1,0:T(8,128)S(1)}, f32[32,128,128]{2,1,0:T(8,128)}, u32[]{:S(2)}) copy-start(f32[32,128,128]{2,1,0:T(8,128)} %get-tuple-element.19.gate0_ref) | copy-start | bytes 6291460
  82.3 39.6 %copy-start.2 = (bf16[2,128,512]{2,1,0:T(8,128)(2,1)S(1)}, bf16[2,128,512]{2,1,0:T(8,128)(2,1)}, u32[]{:S(2)}) copy-start(bf16[2,128,512]{2,1,0:T(8,128)(2,1)} %w_ref.1) | copy-start | bytes 786436
  82.3 39.6 %copy-start.3 = (bf16[2,128,128]{2,1,0:T(8,128)(2,1)S(1)}, bf16[2,128,128]{2,1,0:T(8,128)(2,1)}, u32[]{:S(2)}) copy-start(bf16[2,128,128]{2,1,0:T(8,128)(2,1)} %ow_ref.3) | copy-start | bytes 196612
  82.3 39.6 %copy-start.4 = (bf16[2,128,128]{2,1,0:T(8,128)(2,1)S(1)}, bf16[2,128,128]{2,1,0:T(8,128)(2,1)}, u32[]{:S(2)}) copy-start(bf16[2,128,128]{2,1,0:T(8,128)(2,1)} %g_ref.1) | copy-start | bytes 196612
  82.3 39.6 %copy-start.5 = (s32[1024]{0:T(1024)S(1)}, s32[1024]{0:T(1024)}, u32[]{:S(2)}) copy-start(s32[1024]{0:T(1024)} %token_ref.1) | copy-start | bytes 12292
  82.4 39.6 %copy-start.6 = (f32[2,128]{1,0:T(2,128)S(1)}, f32[2,128]{1,0:T(2,128)}, u32[]{:S(2)}) copy-start(f32[2,128]{1,0:T(2,128)} %gain_ref.1) | copy-start | bytes 3076
  82.4 39.6 %copy-start.7 = (f32[2,128]{1,0:T(2,128)S(1)}, f32[2,128]{1,0:T(2,128)}, u32[]{:S(2)}) copy-start(f32[2,128]{1,0:T(2,128)} %bias_ref.1) | copy-start | bytes 3076
  82.4 39.6 %copy-start.8 = (f32[2,128]{1,0:T(2,128)S(1)}, f32[2,128]{1,0:T(2,128)}, u32[]{:S(2)}) copy-start(f32[2,128]{1,0:T(2,128)} %mgain_ref.3) | copy-start | bytes 3076
  82.4 39.6 %copy-start.9 = (f32[2,128]{1,0:T(2,128)S(1)}, f32[2,128]{1,0:T(2,128)}, u32[]{:S(2)}) copy-start(f32[2,128]{1,0:T(2,128)} %mbias_ref.3) | copy-start | bytes 3076
  191.5 2.7 %collective-permute-start.1 = (bf16[512,1024]{1,0:T(8,128)(2,1)S(1)}, bf16[512,1024]{1,0:T(8,128)(2,1)S(1)}, u32[]{:S(2)}, u32[]{:S(2)}) collective-permute-start(bf16[512,1024]{1,0:T(8,128)(2,1)S(1)} %get-tuple-element.21.l_ref), channel_id=1, source_target_pairs={{0,1},{1,0},{2,3},{3,2},{4,5},{5,4},{6,7},{7,6},{8,9},{9,8},{10,11... | collective-permute-start | bytes 3145736 | tf_op jit(solution)/shard_map/ppermute | solution.py:345

commit v3 on v2

--- a/solution.py
+++ b/solution.py
@@ -10,6 +10,8 @@
 C = 128
 T = 64
 H = 32
+PITCH = 24
+WIDE = 72
 BLK = 16
 VMEM_LIMIT = 24 * 1024 * 1024
 FIRST_LIMIT = 56 * 1024 * 1024
@@ -52,6 +54,10 @@
     shape = (C, C)
     eye = lax.broadcasted_iota(jnp.int32, shape, 0) == lax.broadcasted_iota(jnp.int32, shape, 1)
     return jnp.sum(jnp.where(eye, jnp.broadcast_to(row, shape), 0.0), axis=1, keepdims=True)
+
+
+def unpad(ref):
+    return ref[...].reshape(C, PITCH, C)[:, :BLK].astype(BF16)
 
 
 def project_block(load, block, mask, gain, bias, w, g, x_ref, gate_ref, sl_ref, sr_ref):
@@ -69,10 +75,10 @@
         right = sigmoid(p[2 * C : 3 * C]) * p[3 * C :]
         for u in range(2):
             keep = mask(s + u)
-            sl_ref[:, t + u, :] = left[:, u * C : (u + 1) * C] * keep
-            sr_ref[:, t + u, :] = right[:, u * C : (u + 1) * C] * keep
-    x_ref[:, pl.ds(pl.multiple_of(block * BLK, BLK), BLK), :] = sl_ref[...].astype(BF16)
-    x_ref[:, pl.ds(pl.multiple_of(H + block * BLK, BLK), BLK), :] = sr_ref[...].astype(BF16)
+            sl_ref[pl.ds(t + u, C, stride=PITCH), :] = left[:, u * C : (u + 1) * C] * keep
+            sr_ref[pl.ds(t + u, C, stride=PITCH), :] = right[:, u * C : (u + 1) * C] * keep
+    x_ref[:, pl.ds(pl.multiple_of(block * BLK, BLK), BLK), :] = unpad(sl_ref)
+    x_ref[:, pl.ds(pl.multiple_of(H + block * BLK, BLK), BLK), :] = unpad(sr_ref)
 
 
 def first_kernel(
@@ -126,10 +132,10 @@
     average = jnp.sum(y, axis=0) * (1.0 / C)
     centred = y - average[None]
     spread = jnp.sum(centred * centred, axis=0) * (1.0 / C)
-    s_ref[...] = centred * lax.rsqrt(spread + 1e-05)[None]
+    s_ref[: C * BLK] = (centred * lax.rsqrt(spread + 1e-05)[None]).reshape(C * BLK, C)
     for t in range(BLK):
         s = block * BLK + t
-        normed = (s_ref[:, t, :] * gain + bias).astype(BF16)
+        normed = (s_ref[pl.ds(t, C, stride=BLK), :] * gain + bias).astype(BF16)
         update = lax.dot_general(
             normed, ow, (((0,), (0,)), ((), ())), preferred_element_type=F32
         )
@@ -138,7 +144,7 @@
 
 def middle_kernel(
     y_ref, z_ref, gate0_ref, mgain_ref, mbias_ref, ow_ref, token_ref, mask_ref, gain_ref, bias_ref,
-    w_ref, g_ref, x_ref, gate_ref, zn_ref, sl_ref, sr_ref,
+    w_ref, g_ref, x_ref, gate_ref, zn_ref, sl_ref, sr_ref, zp_ref,
 ):
     mgain, mbias = column(mgain_ref[0:1]), column(mbias_ref[0:1])
     gain, bias = gain_ref[1:2], bias_ref[1:2]
@@ -146,8 +152,10 @@
     start = col_block() * T
 
     def emit(s, change):
-        zn_ref[s] = z_ref[s] + change[:T]
-        zn_ref[s + H] = z_ref[s + H] + change[T:]
+        for i, part in ((s, change[:T]), (s + H, change[T:])):
+            value = z_ref[i] + part
+            zn_ref[i] = value
+            zp_ref[pl.ds(pl.multiple_of(i * WIDE, 8), T), :] = value
 
     def body(block, carry):
         update_block(block, y_ref, mgain, mbias, ow_ref[0], gate0_ref, sl_ref, emit)
@@ -157,20 +165,29 @@
 
     for block in range(H // BLK):
         project_block(
-            lambda s: zn_ref[:, s, :], block, lambda s: line_mask(token_ref, start, s, across), gain, bias,
+            lambda s: zp_ref[pl.ds(s, T, stride=WIDE), :], block, lambda s: line_mask(token_ref, start, s, across), gain, bias,
             w_ref[1], g_ref[1], x_ref, gate_ref, sl_ref, sr_ref,
         )
 
 
-def last_kernel(y_ref, z_ref, gate_ref, mgain_ref, mbias_ref, ow_ref, out_ref, s_ref):
+def last_kernel(y_ref, z_ref, gate_ref, mgain_ref, mbias_ref, ow_ref, out_hbm, s_ref, c_ref, out_ref, sem):
     mgain, mbias = column(mgain_ref[1:2]), column(mbias_ref[1:2])
 
     def emit(s, change):
-        out_ref[:, s, :] = z_ref[:, s, :] + change[:T]
-        out_ref[:, s + H, :] = z_ref[:, s + H, :] + change[T:]
+        c_ref[pl.ds(s, T, stride=WIDE), :] = change[:T]
+        c_ref[pl.ds(s + H, T, stride=WIDE), :] = change[T:]
 
     for block in range(H // BLK):
         update_block(block, y_ref, mgain, mbias, ow_ref[1], gate_ref, s_ref, emit)
+    copies = []
+    for part in range(4):
+        for i in range(part * 16, (part + 1) * 16):
+            out_ref[i] = z_ref[i] + c_ref[i * WIDE : i * WIDE + T]
+        lines = pl.ds(part * 16, 16)
+        copies.append(pltpu.make_async_copy(out_ref.at[lines], out_hbm.at[lines], sem.at[part]))
+        copies[-1].start()
+    for copy in copies:
+        copy.wait()
 
 
 def sides(x0, x1):
@@ -311,7 +328,8 @@
     gates = ((H, 2 * T, C), F32)
     wide = ((C, T, 2 * T), BF16)
     narrow = ((C, H, 2 * T), BF16)
-    line = ((C, BLK, 2 * T), F32)
+    line = ((C * PITCH, 2 * T), F32)
+    tile = ((T * WIDE, C), F32)
 
     x, gate0 = call(
         first_kernel,
@@ -336,7 +354,7 @@
     got = lax.ppermute(other, "core", SWAP)
     (y,) = call(outgoing_sum_kernel, [narrow])(left, right, got)
     y = exchange(y)
-    x, gate1, current = call(middle_kernel, [wide, gates, ((T, T, C), F32)], [line, line], [VMEM_SPEC] * 6 + [SMEM_SPEC] + [VMEM_SPEC] * 5)(
+    x, gate1, current = call(middle_kernel, [wide, gates, ((T, T, C), F32)], [line, line, tile], [VMEM_SPEC] * 6 + [SMEM_SPEC] + [VMEM_SPEC] * 5)(
         y, pair, gate0, mid_gain, mid_bias, out_weight,
         token_mask, mask, in_gain, in_bias, proj_weight, gate_weight,
     )
@@ -346,7 +364,13 @@
     (half,) = call(incoming_own_kernel, [narrow])(left, right)
     (y,) = call(incoming_sum_kernel, [narrow])(got, right, half)
     y = exchange(y)
-    (out,) = call(last_kernel, [((T, T, C), F32)], [line])(
+    (out,) = call(
+        last_kernel,
+        [((T, T, C), F32)],
+        [line, tile, ((T, T, C), F32), pltpu.SemaphoreType.DMA((4,))],
+        [VMEM_SPEC] * 6,
+        [HBM_SPEC],
+    )(
         y, current, gate1, mid_gain, mid_bias, out_weight
     )
     return out

time: 240 us -> 232 us (0.967)
  Pallas kernels: 33.7 us -> 25.5 us
    pallas_call x2, Pallas kernels: 15.4 us -> 9.23 us  [the longest x1 5.68 us: on_device(): call(middle_kernel, [wide, gates, ((T, T, C), F32)], [line, line, tile],...]
where the time goes in v3:
time: 232 us
  blocking collectives  203 us (88%)
  Pallas kernels  25.5 us (11%)
  waiting for transfers between devices  3.04 us (1%)
    all_to_all x4, blocking collectives, exchange(): return lax.all_to_all(x, CHIPS, split_axis=0, concat_axis=0, tiled=True)  203 us
    pallas_call x1, Pallas kernels, on_device(): call(first_kernel, [wide, gates], [line, line, ((T, T, C), F32), pltpu.SM...  5.93 us
    pallas_call x1, Pallas kernels, on_device(): call(middle_kernel, [wide, gates, ((T, T, C), F32)], [line, line, tile],...  5.68 us
  transfers between devices with their start and end apart: 2, of which 2 were waited for; matrix products, arithmetic and copies ran while one was open for 0% of the time, Pallas kernels for 1%

profile of v3, /device:TPU:32, one launch (start us, length us, event | category | flops | bytes accessed | tf_op | source)
XLA Modules:
  0.0 232.2 jit_solution(17875640392719474146)
XLA Ops:
  0.0 5.9 %shard_map.91 = (bf16[128,64,128]{2,1,0:T(8,128)(2,1)}, f32[32,128,128]{2,1,0:T(8,128)}) custom-call(f32[64,64,128]{2,1,0:T(8,128)} %z_ref.1, s32[1024]{0:T(1024)} %token_ref.1, s32[1,1024]{1,0:T(1,128)} %bitcast.1, f32[2,128]{1,0:T(2,128)} %gain_ref.1, f32[2,128]{1,0:T(2,128)} %bias_ref.1, bf16[2,128,512]{2,1,0:T(8,128)(2,1)} %w_ref.1, ...), custom_call_target="tpu_custom_call" | custom-call | tf_op jit(solution)/shard_map/pallas_call | solution.py:334
  5.9 68.5 %all_to_all.20.x_ref = bf16[128,64,128]{2,1,0:T(8,128)(2,1)S(1)} all-to-all(bf16[128,64,128]{2,1,0:T(8,128)(2,1)} %get-tuple-element.15), channel_id=1, replica_groups=mesh['z'=8,'yl'=2,'x'=4,'yh'=2,'core'=2] {'z','yh','yl','x'}, dimensions={0} | all-to-all | bytes 4194304 | tf_op jit(solution)/shard_map/all_to_all | solution.py:321
  74.4 3.1 %shard_map.92 = (bf16[1024,512]{1,0:T(8,128)(2,1)S(1)}, bf16[512,512]{1,0:T(8,128)(2,1)S(1)}, bf16[1024,512]{1,0:T(8,128)(2,1)S(1)}) custom-call(bf16[128,64,128]{2,1,0:T(8,128)(2,1)S(1)} %all_to_all.20.x_ref), custom_call_target="tpu_custom_call" | custom-call | tf_op jit(solution)/shard_map/pallas_call | solution.py:349
  77.5 0.1 collective-permute-start
  77.6 2.6 %collective-permute-done.got_ref = bf16[1024,512]{1,0:T(8,128)(2,1)S(1)} collective-permute-done((bf16[1024,512]{1,0:T(8,128)(2,1)S(1)}, bf16[1024,512]{1,0:T(8,128)(2,1)S(1)}, u32[]{:S(2)}, u32[]{:S(2)}) %collective-permute-start) | collective-permute-done | bytes 1048608 | tf_op jit(solution)/shard_map/ppermute | solution.py:354
  80.2 0.0 copy-start.4
  80.2 0.0 copy-start.5
  80.3 0.0 copy-start.6
  80.3 0.0 copy-start.7
  80.3 0.0 copy-start.8
  80.3 0.0 copy-start.9
  80.3 1.6 shard_map.93
  82.0 37.9 %all_to_all.21.y_ref = bf16[128,32,128]{2,1,0:T(8,128)(2,1)S(1)} all-to-all(bf16[128,32,128]{2,1,0:T(8,128)(2,1)S(1)} %shard_map.93), channel_id=1, replica_groups=mesh['z'=8,'yl'=2,'x'=4,'yh'=2,'core'=2] {'z','yh','yl','x'}, dimensions={0} | all-to-all | bytes 2097152 | tf_op jit(solution)/shard_map/all_to_all | solution.py:321
  119.8 0.0 copy-done
  119.8 0.0 copy-done.1
  119.8 0.0 copy-done.2
  119.8 0.0 copy-done.3
  119.8 0.0 copy-done.4
  119.8 0.0 copy-done.5
  119.8 0.0 copy-done.6
  119.9 0.0 copy-done.7
  119.9 0.0 copy-done.8
  119.9 0.0 copy-done.9
  119.9 5.7 %shard_map.94 = (bf16[128,64,128]{2,1,0:T(8,128)(2,1)S(1)}, f32[32,128,128]{2,1,0:T(8,128)S(1)}, f32[64,64,128]{2,1,0:T(8,128)S(1)}) custom-call(bf16[128,32,128]{2,1,0:T(8,128)(2,1)S(1)} %all_to_all.21.y_ref, f32[64,64,128]{2,1,0:T(8,128)S(1)} %copy-done, f32[32,128,128]{2,1,0:T(8,128)S(1)} %copy-done.1, f32[2,128]{1,0:T(2,128)S(1)} %copy-done.8, ...), custom_call_target="tpu_custom_call" | custom-call | tf_op jit(solution)/shard_map/pallas_call | solution.py:357
  125.6 58.8 %all_to_all.22.x_ref = bf16[128,64,128]{2,1,0:T(8,128)(2,1)S(1)} all-to-all(bf16[128,64,128]{2,1,0:T(8,128)(2,1)S(1)} %get-tuple-element.20), channel_id=1, replica_groups=mesh['z'=8,'yl'=2,'x'=4,'yh'=2,'core'=2] {'z','yh','yl','x'}, dimensions={0} | all-to-all | bytes 4194304 | tf_op jit(solution)/shard_map/all_to_all | solution.py:321
  184.4 1.1 shard_map.95
  185.6 0.1 collective-permute-start.1
  185.7 2.2 shard_map.96.half_ref
  187.9 0.4 collective-permute-done.1.l_ref
  188.3 2.3 shard_map.97
  190.6 37.8 %all_to_all.23.y_ref = bf16[128,32,128]{2,1,0:T(8,128)(2,1)S(1)} all-to-all(bf16[128,32,128]{2,1,0:T(8,128)(2,1)S(1)} %shard_map.97), channel_id=1, replica_groups=mesh['z'=8,'yl'=2,'x'=4,'yh'=2,'core'=2] {'z','yh','yl','x'}, dimensions={0} | all-to-all | bytes 2097152 | tf_op jit(solution)/shard_map/all_to_all | solution.py:321
  228.4 3.5 %shard_map.98 = f32[64,64,128]{2,1,0:T(8,128)} custom-call(bf16[128,32,128]{2,1,0:T(8,128)(2,1)S(1)} %all_to_all.23.y_ref, f32[64,64,128]{2,1,0:T(8,128)S(1)} %get-tuple-element.23.z_ref, f32[32,128,128]{2,1,0:T(8,128)S(1)} %get-tuple-element.24.gate_ref, f32[2,128]{1,0:T(2,128)S(1)} %copy-done.8, f32[2,128]{1,0:T(2,128)S(1)} %copy-done.9, ...), custom_call_target="tpu_custom_call" | custom-call | tf_op jit(solution)/shard_map/pallas_call | solution.py:367
  (4 shorter events, 0.0 us)
Async XLA Ops:
  77.5 2.7 %collective-permute-start = (bf16[1024,512]{1,0:T(8,128)(2,1)S(1)}, bf16[1024,512]{1,0:T(8,128)(2,1)S(1)}, u32[]{:S(2)}, u32[]{:S(2)}) collective-permute-start(bf16[1024,512]{1,0:T(8,128)(2,1)S(1)} %get-tuple-element.18), channel_id=1, source_target_pairs={{0,1},{1,0},{2,3},{3,2},{4,5},{5,4},{6,7},{7,6},{8,9},{9,8},{10,11... | collective-permute-start | bytes 3145736 | tf_op jit(solution)/shard_map/ppermute | solution.py:354
  80.2 39.6 %copy-start = (f32[64,64,128]{2,1,0:T(8,128)S(1)}, f32[64,64,128]{2,1,0:T(8,128)}, u32[]{:S(2)}) copy-start(f32[64,64,128]{2,1,0:T(8,128)} %z_ref.1) | copy-start | bytes 6291460
  80.2 39.6 %copy-start.1 = (f32[32,128,128]{2,1,0:T(8,128)S(1)}, f32[32,128,128]{2,1,0:T(8,128)}, u32[]{:S(2)}) copy-start(f32[32,128,128]{2,1,0:T(8,128)} %get-tuple-element.19.gate0_ref) | copy-start | bytes 6291460
  80.2 39.6 %copy-start.2 = (bf16[2,128,512]{2,1,0:T(8,128)(2,1)S(1)}, bf16[2,128,512]{2,1,0:T(8,128)(2,1)}, u32[]{:S(2)}) copy-start(bf16[2,128,512]{2,1,0:T(8,128)(2,1)} %w_ref.1) | copy-start | bytes 786436
  80.2 39.6 %copy-start.3 = (bf16[2,128,128]{2,1,0:T(8,128)(2,1)S(1)}, bf16[2,128,128]{2,1,0:T(8,128)(2,1)}, u32[]{:S(2)}) copy-start(bf16[2,128,128]{2,1,0:T(8,128)(2,1)} %ow_ref.3) | copy-start | bytes 196612
  80.2 39.6 %copy-start.4 = (bf16[2,128,128]{2,1,0:T(8,128)(2,1)S(1)}, bf16[2,128,128]{2,1,0:T(8,128)(2,1)}, u32[]{:S(2)}) copy-start(bf16[2,128,128]{2,1,0:T(8,128)(2,1)} %g_ref.1) | copy-start | bytes 196612
  80.2 39.6 %copy-start.5 = (s32[1024]{0:T(1024)S(1)}, s32[1024]{0:T(1024)}, u32[]{:S(2)}) copy-start(s32[1024]{0:T(1024)} %token_ref.1) | copy-start | bytes 12292
  80.3 39.6 %copy-start.6 = (f32[2,128]{1,0:T(2,128)S(1)}, f32[2,128]{1,0:T(2,128)}, u32[]{:S(2)}) copy-start(f32[2,128]{1,0:T(2,128)} %gain_ref.1) | copy-start | bytes 3076
  80.3 39.6 %copy-start.7 = (f32[2,128]{1,0:T(2,128)S(1)}, f32[2,128]{1,0:T(2,128)}, u32[]{:S(2)}) copy-start(f32[2,128]{1,0:T(2,128)} %bias_ref.1) | copy-start | bytes 3076
  80.3 39.6 %copy-start.8 = (f32[2,128]{1,0:T(2,128)S(1)}, f32[2,128]{1,0:T(2,128)}, u32[]{:S(2)}) copy-start(f32[2,128]{1,0:T(2,128)} %mgain_ref.3) | copy-start | bytes 3076
  80.3 39.6 %copy-start.9 = (f32[2,128]{1,0:T(2,128)S(1)}, f32[2,128]{1,0:T(2,128)}, u32[]{:S(2)}) copy-start(f32[2,128]{1,0:T(2,128)} %mbias_ref.3) | copy-start | bytes 3076
  185.6 2.7 %collective-permute-start.1 = (bf16[512,1024]{1,0:T(8,128)(2,1)S(1)}, bf16[512,1024]{1,0:T(8,128)(2,1)S(1)}, u32[]{:S(2)}, u32[]{:S(2)}) collective-permute-start(bf16[512,1024]{1,0:T(8,128)(2,1)S(1)} %get-tuple-element.21.l_ref), channel_id=1, source_target_pairs={{0,1},{1,0},{2,3},{3,2},{4,5},{5,4},{6,7},{7,6},{8,9},{9,8},{10,11... | collective-permute-start | bytes 3145736 | tf_op jit(solution)/shard_map/ppermute | solution.py:363

commit v4 on v3

--- a/solution.py
+++ b/solution.py
@@ -133,13 +133,13 @@
     centred = y - average[None]
     spread = jnp.sum(centred * centred, axis=0) * (1.0 / C)
     s_ref[: C * BLK] = (centred * lax.rsqrt(spread + 1e-05)[None]).reshape(C * BLK, C)
-    for t in range(BLK):
-        s = block * BLK + t
-        normed = (s_ref[pl.ds(t, C, stride=BLK), :] * gain + bias).astype(BF16)
-        update = lax.dot_general(
-            normed, ow, (((0,), (0,)), ((), ())), preferred_element_type=F32
-        )
-        emit(s, gate_ref[s] * update)
+    for t in range(0, BLK, 4):
+        lines = jnp.concatenate([s_ref[pl.ds(t + u, C, stride=BLK), :] for u in range(4)], axis=1)
+        normed = (lines * gain + bias).astype(BF16)
+        update = lax.dot_general(normed, ow, (((0,), (0,)), ((), ())), preferred_element_type=F32)
+        for u in range(4):
+            s = block * BLK + t + u
+            emit(s, gate_ref[s] * update[u * C : (u + 1) * C])
 
 
 def middle_kernel(
@@ -157,12 +157,8 @@
             zn_ref[i] = value
             zp_ref[pl.ds(pl.multiple_of(i * WIDE, 8), T), :] = value
 
-    def body(block, carry):
+    for block in range(H // BLK):
         update_block(block, y_ref, mgain, mbias, ow_ref[0], gate0_ref, sl_ref, emit)
-        return carry
-
-    lax.fori_loop(0, H // BLK, body, 0)
-
     for block in range(H // BLK):
         project_block(
             lambda s: zp_ref[pl.ds(s, T, stride=WIDE), :], block, lambda s: line_mask(token_ref, start, s, across), gain, bias,
@@ -204,85 +200,77 @@
     return lax.div(row, 2) * 16 + lax.rem(col, 2) * 8 + lax.rem(row, 2) * 4 + lax.div(col, 2)
 
 
-def outgoing_kernel(x_ref, l_ref, r_ref, other_ref, rs_ref):
-    core = lax.axis_index("core")
-
-    def gather(row, carry):
-        at = pl.multiple_of(row * T, T)
-        to = pl.multiple_of(lax.rem(row, 2) * 512 + lax.div(row, 2) * T, T)
-        base = chip(row, 0)
+def spread_rows(to_ref, at, cols, x0, x1):
+    low, high = sides(x0, x1)
+    to_ref[pl.ds(at, H), cols] = low
+    to_ref[pl.ds(at + H, H), cols] = high
+
+
+def gather_right(x_ref, parity, to_ref):
+    for m in range(8):
         for q in range(4):
-            low, high = sides(x_ref[base + q], x_ref[base + 8 + q])
+            base = m * 16 + parity * 4 + q
+            spread_rows(to_ref, m * T, slice(q * 128, (q + 1) * 128), x_ref[base, H:], x_ref[base + 8, H:])
+
+
+def outgoing_other_kernel(x_ref, l_ref, other_ref, rs_ref):
+    gather_right(x_ref, 1 - lax.axis_index("core"), rs_ref)
+    for row in range(16):
+        for q in range(4):
+            base = (row // 2) * 16 + (row % 2) * 4 + q
+            spread_rows(l_ref, row * T, slice(q * 128, (q + 1) * 128), x_ref[base, :H], x_ref[base + 8, :H])
+    for i in range(2):
+        rows = slice(i * 512, (i + 1) * 512)
+        other_ref[rows, :] = nt_dot(l_ref[rows, :], rs_ref[...]).astype(BF16)
+
+
+def outgoing_own_kernel(x_ref, l_ref, own_ref, rs_ref):
+    gather_right(x_ref, lax.axis_index("core"), rs_ref)
+    for i in range(2):
+        rows = slice(i * 512, (i + 1) * 512)
+        own_ref[rows, :] = nt_dot(l_ref[rows, :], rs_ref[...])
+
+
+def outgoing_sum_kernel(own_ref, got_ref, y_ref):
+    for row in range(16):
+        rows = slice(row * T, (row + 1) * T)
+        total = (own_ref[rows, :] + got_ref[rows, :].astype(F32)).astype(BF16)
+        base = (row // 2) * 16 + (row % 2) * 4
+        for q in range(4):
+            part = total[:, q * 128 : (q + 1) * 128]
+            first, second = sides(part[:H], part[H:])
+            y_ref[base + q] = first
+            y_ref[base + 8 + q] = second
+
+
+def incoming_left_kernel(x_ref, l_ref):
+    for c in range(8):
+        base = (c % 2) * 8 + c // 2
+        for q in range(8):
             cols = slice(q * 128, (q + 1) * 128)
-            l_ref[pl.ds(at, H), cols] = low[:H]
-            l_ref[pl.ds(at + H, H), cols] = high[:H]
-            rs_ref[pl.ds(to, H), cols] = low[H:]
-            rs_ref[pl.ds(to + H, H), cols] = high[H:]
-        return carry
-
-    lax.fori_loop(0, 16, gather, 0)
-    r_ref[...] = rs_ref[pl.ds(pl.multiple_of(core * 512, 512), 512), :]
-    send = rs_ref[pl.ds(pl.multiple_of((1 - core) * 512, 512), 512), :]
-
-    def multiply(i, carry):
-        rows = pl.ds(pl.multiple_of(i * 256, 256), 256)
-        other_ref[rows, :] = nt_dot(l_ref[rows, :], send).astype(BF16)
-        return carry
-
-    lax.fori_loop(0, 4, multiply, 0)
-
-
-def outgoing_sum_kernel(l_ref, r_ref, got_ref, y_ref):
-    def body(i, carry):
-        rows = pl.ds(pl.multiple_of(i * 256, 256), 256)
-        total = (nt_dot(l_ref[rows, :], r_ref[...]) + got_ref[rows, :].astype(F32)).astype(BF16)
-        for b in range(4):
-            base = chip(i * 4 + b, 0)
-            for q in range(4):
-                part = total[b * T : (b + 1) * T, q * 128 : (q + 1) * 128]
-                first, second = sides(part[:H], part[H:])
-                y_ref[base + q] = first
-                y_ref[base + 8 + q] = second
-        return carry
-
-    lax.fori_loop(0, 4, body, 0)
-
-
-def incoming_kernel(x_ref, l_ref, r_ref):
-    def gather(c, carry):
-        at = pl.multiple_of(c * T, T)
-        base = chip(0, c)
+            spread_rows(l_ref, c * T, cols, x_ref[16 * q + base, :H], x_ref[16 * q + 4 + base, :H])
+
+
+def incoming_half(l_ref, r_ref, write):
+    total = nt_dot(r_ref[...], l_ref[...]).astype(BF16)
+    for c in range(8):
+        base = (c % 2) * 8 + c // 2
+        for q in range(4):
+            part = total[c * T : (c + 1) * T, q * 128 : (q + 1) * 128]
+            first, second = sides(part[:H], part[H:])
+            write(2 * q, base, first)
+            write(2 * q + 1, base, second)
+
+
+def incoming_own_kernel(x_ref, l_ref, r_ref, half_ref):
+    for c in range(8):
+        base = (c % 2) * 8 + c // 2
         for q in range(8):
-            low, high = sides(x_ref[16 * q + base], x_ref[16 * q + 4 + base])
             cols = slice(q * 128, (q + 1) * 128)
-            l_ref[pl.ds(at, H), cols] = low[:H]
-            l_ref[pl.ds(at + H, H), cols] = high[:H]
-            r_ref[pl.ds(at, H), cols] = low[H:]
-            r_ref[pl.ds(at + H, H), cols] = high[H:]
-        return carry
-
-    lax.fori_loop(0, 8, gather, 0)
-
-
-def incoming_half(l_ref, r_ref, write):
-    def body(i, carry):
-        right = r_ref[pl.ds(pl.multiple_of(i * 128, 128), 128), :]
-        total = nt_dot(right, l_ref[...]).astype(BF16)
-        for b in range(2):
-            base = chip(0, i * 2 + b)
-            for q in range(4):
-                part = total[b * T : (b + 1) * T, q * 128 : (q + 1) * 128]
-                first, second = sides(part[:H], part[H:])
-                write(2 * q, base, first)
-                write(2 * q + 1, base, second)
-        return carry
-
-    lax.fori_loop(0, 4, body, 0)
-
-
-def incoming_own_kernel(l_ref, r_ref, half_ref):
+            spread_rows(r_ref, c * T, cols, x_ref[16 * q + base, H:], x_ref[16 * q + 4 + base, H:])
+
     def write(plane, base, value):
-        half_ref[plane * 16 + base] = value
+        half_ref[plane * 8 + base // 8 * 4 + base % 4] = value
 
     incoming_half(l_ref, r_ref, write)
 
@@ -296,7 +284,7 @@
     incoming_half(l_ref, r_ref, write)
     for plane in range(8):
         for y in range(2):
-            y_ref[pl.ds(plane * 16 + y * 8 + own * 4, 4)] = half_ref[pl.ds(plane * 16 + y * 8, 4)]
+            y_ref[pl.ds(plane * 16 + y * 8 + own * 4, 4)] = half_ref[plane * 8 + y * 4 : plane * 8 + y * 4 + 4]
 
 
 def call(kernel, outs, scratch=(), specs=None, out_specs=None, limit=VMEM_LIMIT):
@@ -346,22 +334,21 @@
         pair, token_mask, mask, in_gain, in_bias, proj_weight, gate_weight
     )
     x = exchange(x)
-    left, right, other = call(
-        outgoing_kernel,
-        [((1024, 512), BF16), ((512, 512), BF16), ((1024, 512), BF16)],
-        [((1024, 512), BF16)],
-    )(x)
+    right = ((512, 512), BF16)
+    left, other = call(outgoing_other_kernel, [((1024, 512), BF16), ((1024, 512), BF16)], [right])(x)
     got = lax.ppermute(other, "core", SWAP)
-    (y,) = call(outgoing_sum_kernel, [narrow])(left, right, got)
+    (own,) = call(outgoing_own_kernel, [((1024, 512), F32)], [right])(x, left)
+    (y,) = call(outgoing_sum_kernel, [narrow])(own, got)
     y = exchange(y)
     x, gate1, current = call(middle_kernel, [wide, gates, ((T, T, C), F32)], [line, line, tile], [VMEM_SPEC] * 6 + [SMEM_SPEC] + [VMEM_SPEC] * 5)(
         y, pair, gate0, mid_gain, mid_bias, out_weight,
         token_mask, mask, in_gain, in_bias, proj_weight, gate_weight,
     )
     x = exchange(x)
-    left, right = call(incoming_kernel, [((512, 1024), BF16), ((512, 1024), BF16)])(x)
+    side = ((512, 1024), BF16)
+    (left,) = call(incoming_left_kernel, [side])(x)
     got = lax.ppermute(left, "core", SWAP)
-    (half,) = call(incoming_own_kernel, [narrow])(left, right)
+    right, half = call(incoming_own_kernel, [side, ((64, H, 2 * T), BF16)])(x, left)
     (y,) = call(incoming_sum_kernel, [narrow])(got, right, half)
     y = exchange(y)
     (out,) = call(

time: 232 us -> 227 us (0.978)
  Pallas kernels: 25.5 us -> 19.1 us
    pallas_call x4 -> x5, Pallas kernels: 8.09 us -> 3.3 us  [the longest x1 0.89 us: on_device(): call(outgoing_other_kernel, [((1024, 512), BF16), ((1024, 512), BF16)], [...]
where the time goes in v4:
time: 227 us; the launch traced here: 226 us
  blocking collectives  203 us (89%)
  Pallas kernels  19.1 us (8%)
  waiting for transfers between devices  3.57 us (2%)
    all_to_all x4, blocking collectives, exchange(): return lax.all_to_all(x, CHIPS, split_axis=0, concat_axis=0, tiled=True)  203 us
    pallas_call x1, Pallas kernels, on_device(): call(first_kernel, [wide, gates], [line, line, ((T, T, C), F32), pltpu.SM...  5.93 us
    pallas_call x1, Pallas kernels, on_device(): call(middle_kernel, [wide, gates, ((T, T, C), F32)], [line, line, tile],...  5.6 us
  transfers between devices with their start and end apart: 2, of which 2 were waited for; matrix products, arithmetic and copies ran while one was open for 0% of the time, Pallas kernels for 1%

profile of v4, /device:TPU:32, one launch (start us, length us, event | category | flops | bytes accessed | tf_op | source)
XLA Modules:
  0.0 226.3 jit_solution(6919698816948778431)
XLA Ops:
  0.0 5.9 %shard_map.91 = (bf16[128,64,128]{2,1,0:T(8,128)(2,1)}, f32[32,128,128]{2,1,0:T(8,128)}) custom-call(f32[64,64,128]{2,1,0:T(8,128)} %z_ref.1, s32[1024]{0:T(1024)} %token_ref.1, s32[1,1024]{1,0:T(1,128)} %bitcast.1, f32[2,128]{1,0:T(2,128)} %gain_ref.1, f32[2,128]{1,0:T(2,128)} %bias_ref.1, bf16[2,128,512]{2,1,0:T(8,128)(2,1)} %w_ref.1, ...), custom_call_target="tpu_custom_call" | custom-call | tf_op jit(solution)/shard_map/pallas_call | solution.py:322
  5.9 68.5 %all_to_all.20.x_ref = bf16[128,64,128]{2,1,0:T(8,128)(2,1)S(1)} all-to-all(bf16[128,64,128]{2,1,0:T(8,128)(2,1)} %get-tuple-element.14), channel_id=1, replica_groups=mesh['z'=8,'yl'=2,'x'=4,'yh'=2,'core'=2] {'z','yh','yl','x'}, dimensions={0} | all-to-all | bytes 4194304 | tf_op jit(solution)/shard_map/all_to_all | solution.py:309
  74.4 0.9 shard_map.92
  75.3 0.1 collective-permute-start
  75.4 0.9 shard_map.93.own_ref
  76.3 1.8 collective-permute-done.got_ref
  78.1 0.0 copy-start.5
  78.1 0.0 copy-start.7
  78.1 0.0 copy-start.8
  78.1 0.0 copy-start.9
  78.1 0.3 shard_map.94
  78.5 0.0 copy-start
  78.5 0.0 copy-start.6
  78.5 38.1 %all_to_all.21.y_ref = bf16[128,32,128]{2,1,0:T(8,128)(2,1)S(1)} all-to-all(bf16[128,32,128]{2,1,0:T(8,128)(2,1)S(1)} %shard_map.94), channel_id=1, replica_groups=mesh['z'=8,'yl'=2,'x'=4,'yh'=2,'core'=2] {'z','yh','yl','x'}, dimensions={0} | all-to-all | bytes 2097152 | tf_op jit(solution)/shard_map/all_to_all | solution.py:309
  116.6 0.0 copy-done.1
  116.6 0.0 copy-done.2
  116.6 0.0 copy-done.3
  116.6 0.0 copy-done.4
  116.6 0.0 copy-done.5
  116.6 0.0 copy-done.7
  116.7 0.0 copy-done.8
  116.7 0.0 copy-done.9
  116.7 0.0 copy-done
  116.7 5.6 %shard_map.95 = (bf16[128,64,128]{2,1,0:T(8,128)(2,1)S(1)}, f32[32,128,128]{2,1,0:T(8,128)S(1)}, f32[64,64,128]{2,1,0:T(8,128)S(1)}) custom-call(bf16[128,32,128]{2,1,0:T(8,128)(2,1)S(1)} %all_to_all.21.y_ref, f32[64,64,128]{2,1,0:T(8,128)S(1)} %copy-done, f32[32,128,128]{2,1,0:T(8,128)S(1)} %copy-done.1, f32[2,128]{1,0:T(2,128)S(1)} %copy-done.8, ...), custom_call_target="tpu_custom_call" | custom-call | tf_op jit(solution)/shard_map/pallas_call | solution.py:343
  122.3 58.7 %all_to_all.22.x_ref = bf16[128,64,128]{2,1,0:T(8,128)(2,1)S(1)} all-to-all(bf16[128,64,128]{2,1,0:T(8,128)(2,1)S(1)} %get-tuple-element.18), channel_id=1, replica_groups=mesh['z'=8,'yl'=2,'x'=4,'yh'=2,'core'=2] {'z','yh','yl','x'}, dimensions={0} | all-to-all | bytes 4194304 | tf_op jit(solution)/shard_map/all_to_all | solution.py:309
  181.0 0.3 shard_map.96.l_ref
  181.3 0.1 collective-permute-start.1
  181.4 0.8 shard_map.97
  182.3 1.8 collective-permute-done.1.l_ref
  184.1 0.8 shard_map.98
  184.9 37.8 %all_to_all.23.y_ref = bf16[128,32,128]{2,1,0:T(8,128)(2,1)S(1)} all-to-all(bf16[128,32,128]{2,1,0:T(8,128)(2,1)S(1)} %shard_map.98), channel_id=1, replica_groups=mesh['z'=8,'yl'=2,'x'=4,'yh'=2,'core'=2] {'z','yh','yl','x'}, dimensions={0} | all-to-all | bytes 2097152 | tf_op jit(solution)/shard_map/all_to_all | solution.py:309
  222.7 3.4 %shard_map.99 = f32[64,64,128]{2,1,0:T(8,128)} custom-call(bf16[128,32,128]{2,1,0:T(8,128)(2,1)S(1)} %all_to_all.23.y_ref, f32[64,64,128]{2,1,0:T(8,128)S(1)} %get-tuple-element.21.z_ref, f32[32,128,128]{2,1,0:T(8,128)S(1)} %get-tuple-element.22.gate_ref, f32[2,128]{1,0:T(2,128)S(1)} %copy-done.8, f32[2,128]{1,0:T(2,128)S(1)} %copy-done.9, ...), custom_call_target="tpu_custom_call" | custom-call | tf_op jit(solution)/shard_map/pallas_call | solution.py:354
  (5 shorter events, 0.0 us)
Async XLA Ops:
  75.3 2.7 %collective-permute-start = (bf16[1024,512]{1,0:T(8,128)(2,1)S(1)}, bf16[1024,512]{1,0:T(8,128)(2,1)S(1)}, u32[]{:S(2)}, u32[]{:S(2)}) collective-permute-start(bf16[1024,512]{1,0:T(8,128)(2,1)S(1)} %get-tuple-element.16), channel_id=1, source_target_pairs={{0,1},{1,0},{2,3},{3,2},{4,5},{5,4},{6,7},{7,6},{8,9},{9,8},{10,11... | collective-permute-start | bytes 3145736 | tf_op jit(solution)/shard_map/ppermute | solution.py:339
  78.1 38.6 %copy-start.1 = (f32[32,128,128]{2,1,0:T(8,128)S(1)}, f32[32,128,128]{2,1,0:T(8,128)}, u32[]{:S(2)}) copy-start(f32[32,128,128]{2,1,0:T(8,128)} %get-tuple-element.17.gate0_ref) | copy-start | bytes 6291460
  78.1 38.6 %copy-start.2 = (bf16[2,128,512]{2,1,0:T(8,128)(2,1)S(1)}, bf16[2,128,512]{2,1,0:T(8,128)(2,1)}, u32[]{:S(2)}) copy-start(bf16[2,128,512]{2,1,0:T(8,128)(2,1)} %w_ref.1) | copy-start | bytes 786436
  78.1 38.6 %copy-start.3 = (bf16[2,128,128]{2,1,0:T(8,128)(2,1)S(1)}, bf16[2,128,128]{2,1,0:T(8,128)(2,1)}, u32[]{:S(2)}) copy-start(bf16[2,128,128]{2,1,0:T(8,128)(2,1)} %ow_ref.3) | copy-start | bytes 196612
  78.1 38.6 %copy-start.4 = (bf16[2,128,128]{2,1,0:T(8,128)(2,1)S(1)}, bf16[2,128,128]{2,1,0:T(8,128)(2,1)}, u32[]{:S(2)}) copy-start(bf16[2,128,128]{2,1,0:T(8,128)(2,1)} %g_ref.1) | copy-start | bytes 196612
  78.1 38.6 %copy-start.5 = (s32[1024]{0:T(1024)S(1)}, s32[1024]{0:T(1024)}, u32[]{:S(2)}) copy-start(s32[1024]{0:T(1024)} %token_ref.1) | copy-start | bytes 12292
  78.1 38.6 %copy-start.7 = (f32[2,128]{1,0:T(2,128)S(1)}, f32[2,128]{1,0:T(2,128)}, u32[]{:S(2)}) copy-start(f32[2,128]{1,0:T(2,128)} %bias_ref.1) | copy-start | bytes 3076
  78.1 38.6 %copy-start.8 = (f32[2,128]{1,0:T(2,128)S(1)}, f32[2,128]{1,0:T(2,128)}, u32[]{:S(2)}) copy-start(f32[2,128]{1,0:T(2,128)} %mgain_ref.3) | copy-start | bytes 3076
  78.1 38.6 %copy-start.9 = (f32[2,128]{1,0:T(2,128)S(1)}, f32[2,128]{1,0:T(2,128)}, u32[]{:S(2)}) copy-start(f32[2,128]{1,0:T(2,128)} %mbias_ref.3) | copy-start | bytes 3076
  78.5 38.2 %copy-start = (f32[64,64,128]{2,1,0:T(8,128)S(1)}, f32[64,64,128]{2,1,0:T(8,128)}, u32[]{:S(2)}) copy-start(f32[64,64,128]{2,1,0:T(8,128)} %z_ref.1) | copy-start | bytes 6291460
  78.5 38.2 %copy-start.6 = (f32[2,128]{1,0:T(2,128)S(1)}, f32[2,128]{1,0:T(2,128)}, u32[]{:S(2)}) copy-start(f32[2,128]{1,0:T(2,128)} %gain_ref.1) | copy-start | bytes 3076
  181.3 2.7 %collective-permute-start.1 = (bf16[512,1024]{1,0:T(8,128)(2,1)S(1)}, bf16[512,1024]{1,0:T(8,128)(2,1)S(1)}, u32[]{:S(2)}, u32[]{:S(2)}) collective-permute-start(bf16[512,1024]{1,0:T(8,128)(2,1)S(1)} %shard_map.96.l_ref), channel_id=1, source_target_pairs={{0,1},{1,0},{2,3},{3,2},{4,5},{5,4},{6,7},{7,6},{8,9},{9,8},{10,11... | collective-permute-start | bytes 3145736 | tf_op jit(solution)/shard_map/ppermute | solution.py:350

commit v5 on v4

--- a/solution.py
+++ b/solution.py
@@ -17,8 +17,13 @@
 FIRST_LIMIT = 56 * 1024 * 1024
 
 
-def sigmoid(x):
-    return 0.5 * jnp.tanh(0.5 * x) + 0.5
+def halved(weights):
+    return (weights.astype(F32) * 0.5).astype(BF16)
+
+
+def gate_weights_halved(w):
+    blocks = [w[:, i * C : (i + 1) * C] for i in range(4)]
+    return jnp.concatenate([halved(blocks[0]), blocks[1], halved(blocks[2]), blocks[3]], axis=1)
 
 
 def layer_norm(values, gain, bias):
@@ -33,7 +38,7 @@
     turned = jnp.concatenate([chunk[:, T:], chunk[:, :T]], axis=1)
     lane = lax.broadcasted_iota(jnp.int32, (1, 2 * T), 1)
     keep = lax.div(lane, T) == lax.rem(block, 2)
-    return jnp.where(keep, chunk, turned)
+    return jnp.where(keep, chunk, turned) * 0.5
 
 
 def line_mask(token_ref, start, s, across):
@@ -57,10 +62,10 @@
 
 
 def unpad(ref):
-    return ref[...].reshape(C, PITCH, C)[:, :BLK].astype(BF16)
-
-
-def project_block(load, block, mask, gain, bias, w, g, x_ref, gate_ref, sl_ref, sr_ref):
+    return ref[: C * PITCH].reshape(C, PITCH, C)[:, :BLK].astype(BF16)
+
+
+def project_block(load, block, mask, gain, bias, w, g, x_ref, keep_gate, sl_ref, sr_ref):
     for t in range(0, BLK, 2):
         s = block * BLK + t
         lines = jnp.concatenate([load(s), load(s + H), load(s + 1), load(s + 1 + H)], axis=0)
@@ -68,11 +73,11 @@
         p = lax.dot_general(
             w, normed, (((0,), (1,)), ((), ())), preferred_element_type=F32
         )
-        gate = sigmoid(jnp.dot(normed, g, preferred_element_type=F32))
-        gate_ref[s] = gate[:C]
-        gate_ref[s + 1] = gate[C:]
-        left = sigmoid(p[:C]) * p[C : 2 * C]
-        right = sigmoid(p[2 * C : 3 * C]) * p[3 * C :]
+        gate = jnp.tanh(jnp.dot(normed, g, preferred_element_type=F32)) + 1.0
+        keep_gate(s, gate[:C])
+        keep_gate(s + 1, gate[C:])
+        left = (jnp.tanh(p[:C]) + 1.0) * p[C : 2 * C]
+        right = (jnp.tanh(p[2 * C : 3 * C]) + 1.0) * p[3 * C :]
         for u in range(2):
             keep = mask(s + u)
             sl_ref[pl.ds(t + u, C, stride=PITCH), :] = left[:, u * C : (u + 1) * C] * keep
@@ -95,39 +100,43 @@
         )
     ]
     parts = []
-    for block in range(H // BLK):
-        for half in range(2):
-            lines = pl.ds(half * H + block * BLK, BLK)
-            parts.append(pltpu.make_async_copy(z_hbm.at[lines], z_ref.at[lines], z_sem.at[len(parts)]))
-    for copy in small + parts:
+    for n in range(T // BLK):
+        lines = pl.ds(n % 2 * H + n // 2 * BLK, BLK)
+        parts.append(pltpu.make_async_copy(z_hbm.at[lines], z_ref.at[lines], z_sem.at[n]))
+    for copy in parts[:2] + small + parts[2:]:
         copy.start()
     for copy in small:
         copy.wait()
     gain, bias = gain_ref[0:1], bias_ref[0:1]
     across = lanes_twice(mask_ref, col_block())
     start = row_block() * T
+    w, g = gate_weights_halved(w_ref[...]), halved(g_ref[...])
     copies = []
+
+    def keep_gate(s, value):
+        gate_ref[s] = value
+
+    def send(source, to):
+        copies.append(pltpu.make_async_copy(source, to, out_sem.at[len(copies)]))
+        copies[-1].start()
+
     for block in range(H // BLK):
         parts[2 * block].wait()
         parts[2 * block + 1].wait()
         project_block(
             lambda s: z_ref[s], block, lambda s: line_mask(token_ref, start, s, across), gain, bias,
-            w_ref[...], g_ref[...], x_ref, gate_ref, sl_ref, sr_ref,
+            w, g, x_ref, keep_gate, sl_ref, sr_ref,
         )
         for half in range(2):
             lines = pl.ds(half * H + block * BLK, BLK)
-            copies.append(
-                pltpu.make_async_copy(x_ref.at[:, lines], x_hbm.at[:, lines], out_sem.at[len(copies)])
-            )
-            copies[-1].start()
+            send(x_ref.at[:, lines], x_hbm.at[:, lines])
         lines = pl.ds(block * BLK, BLK)
-        copies.append(pltpu.make_async_copy(gate_ref.at[lines], gate_hbm.at[lines], out_sem.at[len(copies)]))
-        copies[-1].start()
+        send(gate_ref.at[lines], gate_hbm.at[lines])
     for copy in copies:
         copy.wait()
 
 
-def update_block(block, y_ref, gain, bias, ow, gate_ref, s_ref, emit):
+def update_block(block, y_ref, gain, bias, ow, s_ref, emit):
     y = y_ref[:, pl.ds(pl.multiple_of(block * BLK, BLK), BLK), :].astype(F32)
     average = jnp.sum(y, axis=0) * (1.0 / C)
     centred = y - average[None]
@@ -139,49 +148,52 @@
         update = lax.dot_general(normed, ow, (((0,), (0,)), ((), ())), preferred_element_type=F32)
         for u in range(4):
             s = block * BLK + t + u
-            emit(s, gate_ref[s] * update[u * C : (u + 1) * C])
+            emit(s, update[u * C : (u + 1) * C])
 
 
 def middle_kernel(
     y_ref, z_ref, gate0_ref, mgain_ref, mbias_ref, ow_ref, token_ref, mask_ref, gain_ref, bias_ref,
-    w_ref, g_ref, x_ref, gate_ref, zn_ref, sl_ref, sr_ref, zp_ref,
+    w_ref, g_ref, x_ref, gate_ref, zp_ref, sl_ref, sr_ref,
 ):
     mgain, mbias = column(mgain_ref[0:1]), column(mbias_ref[0:1])
     gain, bias = gain_ref[1:2], bias_ref[1:2]
     across = lanes_twice(mask_ref, row_block())
     start = col_block() * T
-
-    def emit(s, change):
+    w, g = gate_weights_halved(w_ref[1]), halved(g_ref[1])
+
+    def keep_gate(s, value):
+        gate_ref[pl.ds(s, T, stride=WIDE), :] = value[:T]
+        gate_ref[pl.ds(s + H, T, stride=WIDE), :] = value[T:]
+
+    def emit(s, update):
+        change = gate0_ref[s] * update
         for i, part in ((s, change[:T]), (s + H, change[T:])):
-            value = z_ref[i] + part
-            zn_ref[i] = value
-            zp_ref[pl.ds(pl.multiple_of(i * WIDE, 8), T), :] = value
+            zp_ref[pl.ds(pl.multiple_of(i * WIDE, 8), T), :] = z_ref[i] + part
 
     for block in range(H // BLK):
-        update_block(block, y_ref, mgain, mbias, ow_ref[0], gate0_ref, sl_ref, emit)
+        update_block(block, y_ref, mgain, mbias, halved(ow_ref[0]), sl_ref, emit)
     for block in range(H // BLK):
         project_block(
             lambda s: zp_ref[pl.ds(s, T, stride=WIDE), :], block, lambda s: line_mask(token_ref, start, s, across), gain, bias,
-            w_ref[1], g_ref[1], x_ref, gate_ref, sl_ref, sr_ref,
+            w, g, x_ref, keep_gate, sl_ref, sr_ref,
         )
 
 
-def last_kernel(y_ref, z_ref, gate_ref, mgain_ref, mbias_ref, ow_ref, out_hbm, s_ref, c_ref, out_ref, sem):
+def last_kernel(y_ref, z_ref, gate_ref, mgain_ref, mbias_ref, ow_ref, out_hbm, s_ref, out_ref, sem):
     mgain, mbias = column(mgain_ref[1:2]), column(mbias_ref[1:2])
 
-    def emit(s, change):
-        c_ref[pl.ds(s, T, stride=WIDE), :] = change[:T]
-        c_ref[pl.ds(s + H, T, stride=WIDE), :] = change[T:]
-
+    def emit(s, update):
+        for i, part in ((s, update[:T]), (s + H, update[T:])):
+            rows = slice(i * WIDE, i * WIDE + T)
+            out_ref[i] = z_ref[rows, :] + gate_ref[rows, :] * part
+
+    copies = []
     for block in range(H // BLK):
-        update_block(block, y_ref, mgain, mbias, ow_ref[1], gate_ref, s_ref, emit)
-    copies = []
-    for part in range(4):
-        for i in range(part * 16, (part + 1) * 16):
-            out_ref[i] = z_ref[i] + c_ref[i * WIDE : i * WIDE + T]
-        lines = pl.ds(part * 16, 16)
-        copies.append(pltpu.make_async_copy(out_ref.at[lines], out_hbm.at[lines], sem.at[part]))
-        copies[-1].start()
+        update_block(block, y_ref, mgain, mbias, halved(ow_ref[1]), s_ref, emit)
+        for half in range(2):
+            lines = pl.ds(half * H + block * BLK, BLK)
+            copies.append(pltpu.make_async_copy(out_ref.at[lines], out_hbm.at[lines], sem.at[len(copies)]))
+            copies[-1].start()
     for copy in copies:
         copy.wait()
 
@@ -252,14 +264,13 @@
 
 
 def incoming_half(l_ref, r_ref, write):
-    total = nt_dot(r_ref[...], l_ref[...]).astype(BF16)
+    total = nt_dot(l_ref[...], r_ref[...]).astype(BF16)
     for c in range(8):
-        base = (c % 2) * 8 + c // 2
         for q in range(4):
             part = total[c * T : (c + 1) * T, q * 128 : (q + 1) * 128]
             first, second = sides(part[:H], part[H:])
-            write(2 * q, base, first)
-            write(2 * q + 1, base, second)
+            write(c, q, first)
+            write(c, 8 + q, second)
 
 
 def incoming_own_kernel(x_ref, l_ref, r_ref, half_ref):
@@ -316,8 +327,8 @@
     gates = ((H, 2 * T, C), F32)
     wide = ((C, T, 2 * T), BF16)
     narrow = ((C, H, 2 * T), BF16)
-    line = ((C * PITCH, 2 * T), F32)
-    tile = ((T * WIDE, C), F32)
+    line = (((C + 1) * PITCH, 2 * T), F32)
+    tile = (((T + 1) * WIDE, C), F32)
 
     x, gate0 = call(
         first_kernel,
@@ -325,7 +336,7 @@
         [
             line, line, ((T, T, C), F32), pltpu.SMEM((1024,), jnp.int32), ((1, 1024), jnp.int32), ((2, C), F32),
             ((2, C), F32), ((C, 4 * C), BF16), ((C, C), BF16), wide, gates, pltpu.SemaphoreType.DMA((6,)),
-            pltpu.SemaphoreType.DMA((4,)), pltpu.SemaphoreType.DMA((6,)),
+            pltpu.SemaphoreType.DMA((T // BLK,)), pltpu.SemaphoreType.DMA((6,)),
         ],
         [HBM_SPEC] * 7,
         [HBM_SPEC] * 2,
@@ -340,7 +351,7 @@
     (own,) = call(outgoing_own_kernel, [((1024, 512), F32)], [right])(x, left)
     (y,) = call(outgoing_sum_kernel, [narrow])(own, got)
     y = exchange(y)
-    x, gate1, current = call(middle_kernel, [wide, gates, ((T, T, C), F32)], [line, line, tile], [VMEM_SPEC] * 6 + [SMEM_SPEC] + [VMEM_SPEC] * 5)(
+    x, gate1, current = call(middle_kernel, [wide, tile, tile], [line, line], [VMEM_SPEC] * 6 + [SMEM_SPEC] + [VMEM_SPEC] * 5)(
         y, pair, gate0, mid_gain, mid_bias, out_weight,
         token_mask, mask, in_gain, in_bias, proj_weight, gate_weight,
     )
@@ -354,7 +365,7 @@
     (out,) = call(
         last_kernel,
         [((T, T, C), F32)],
-        [line, tile, ((T, T, C), F32), pltpu.SemaphoreType.DMA((4,))],
+        [line, ((T, T, C), F32), pltpu.SemaphoreType.DMA((4,))],
         [VMEM_SPEC] * 6,
         [HBM_SPEC],
     )(

time: 227 us -> 226 us (level)
  no operation moved by 1% of the time
where the time goes in v5:
time: 226 us
  blocking collectives  203 us (90%)
  Pallas kernels  18.5 us (8%)
  waiting for transfers between devices  3.44 us (2%)
    all_to_all x4, blocking collectives, exchange(): return lax.all_to_all(x, CHIPS, split_axis=0, concat_axis=0, tiled=True)  203 us
    pallas_call x1, Pallas kernels, on_device(): call(first_kernel, [wide, gates], [line, line, ((T, T, C), F32), pltpu.SM...  5.74 us
    pallas_call x1, Pallas kernels, on_device(): call(middle_kernel, [wide, tile, tile], [line, line], [VMEM_SPEC] * 6 + [...  5.54 us
  transfers between devices with their start and end apart: 2, of which 2 were waited for; matrix products, arithmetic and copies ran while one was open for 0% of the time, Pallas kernels for 1%

profile of v5, /device:TPU:32, one launch (start us, length us, event | category | flops | bytes accessed | tf_op | source)
XLA Modules:
  0.0 225.6 jit_solution(3569738683983343285)
XLA Ops:
  0.0 5.7 %shard_map.91 = (bf16[128,64,128]{2,1,0:T(8,128)(2,1)}, f32[32,128,128]{2,1,0:T(8,128)}) custom-call(f32[64,64,128]{2,1,0:T(8,128)} %z_ref.1, s32[1024]{0:T(1024)} %token_ref.1, s32[1,1024]{1,0:T(1,128)} %bitcast.1, f32[2,128]{1,0:T(2,128)} %gain_ref.1, f32[2,128]{1,0:T(2,128)} %bias_ref.1, bf16[2,128,512]{2,1,0:T(8,128)(2,1)} %w_ref.1, ...), custom_call_target="tpu_custom_call" | custom-call | tf_op jit(solution)/shard_map/pallas_call | solution.py:333
  5.8 68.5 %all_to_all.20.x_ref = bf16[128,64,128]{2,1,0:T(8,128)(2,1)S(1)} all-to-all(bf16[128,64,128]{2,1,0:T(8,128)(2,1)} %get-tuple-element.14), channel_id=1, replica_groups=mesh['z'=8,'yl'=2,'x'=4,'yh'=2,'core'=2] {'z','yh','yl','x'}, dimensions={0} | all-to-all | bytes 4194304 | tf_op jit(solution)/shard_map/all_to_all | solution.py:320
  74.2 0.9 shard_map.92
  75.1 0.1 collective-permute-start
  75.2 0.9 shard_map.93.own_ref
  76.1 1.8 collective-permute-done.got_ref
  77.9 0.0 copy-start.5
  77.9 0.0 copy-start.7
  77.9 0.0 copy-start.8
  77.9 0.0 copy-start.9
  77.9 0.3 shard_map.94
  78.3 0.0 copy-start
  78.3 0.0 copy-start.6
  78.3 38.1 %all_to_all.21.y_ref = bf16[128,32,128]{2,1,0:T(8,128)(2,1)S(1)} all-to-all(bf16[128,32,128]{2,1,0:T(8,128)(2,1)S(1)} %shard_map.94), channel_id=1, replica_groups=mesh['z'=8,'yl'=2,'x'=4,'yh'=2,'core'=2] {'z','yh','yl','x'}, dimensions={0} | all-to-all | bytes 2097152 | tf_op jit(solution)/shard_map/all_to_all | solution.py:320
  116.4 0.0 copy-done.1
  116.4 0.0 copy-done.2
  116.4 0.0 copy-done.3
  116.4 0.0 copy-done.4
  116.4 0.0 copy-done.5
  116.5 0.0 copy-done.7
  116.5 0.0 copy-done.8
  116.5 0.0 copy-done.9
  116.5 0.0 copy-done
  116.5 5.5 %shard_map.95 = (bf16[128,64,128]{2,1,0:T(8,128)(2,1)S(1)}, f32[4680,128]{1,0:T(8,128)S(1)}, f32[4680,128]{1,0:T(8,128)S(1)}) custom-call(bf16[128,32,128]{2,1,0:T(8,128)(2,1)S(1)} %all_to_all.21.y_ref, f32[64,64,128]{2,1,0:T(8,128)S(1)} %copy-done, f32[32,128,128]{2,1,0:T(8,128)S(1)} %copy-done.1, f32[2,128]{1,0:T(2,128)S(1)} %copy-done.8, ...), custom_call_target="tpu_custom_call" | custom-call | tf_op jit(solution)/shard_map/pallas_call | solution.py:354
  122.1 58.7 %all_to_all.22.x_ref = bf16[128,64,128]{2,1,0:T(8,128)(2,1)S(1)} all-to-all(bf16[128,64,128]{2,1,0:T(8,128)(2,1)S(1)} %get-tuple-element.18), channel_id=1, replica_groups=mesh['z'=8,'yl'=2,'x'=4,'yh'=2,'core'=2] {'z','yh','yl','x'}, dimensions={0} | all-to-all | bytes 4194304 | tf_op jit(solution)/shard_map/all_to_all | solution.py:320
  180.7 0.3 shard_map.96.l_ref
  181.1 0.1 collective-permute-start.1
  181.2 1.0 shard_map.97
  182.1 1.7 collective-permute-done.1.l_ref
  183.8 0.8 shard_map.98
  184.6 37.8 %all_to_all.23.y_ref = bf16[128,32,128]{2,1,0:T(8,128)(2,1)S(1)} all-to-all(bf16[128,32,128]{2,1,0:T(8,128)(2,1)S(1)} %shard_map.98), channel_id=1, replica_groups=mesh['z'=8,'yl'=2,'x'=4,'yh'=2,'core'=2] {'z','yh','yl','x'}, dimensions={0} | all-to-all | bytes 2097152 | tf_op jit(solution)/shard_map/all_to_all | solution.py:320
  222.5 3.0 %shard_map.99 = f32[64,64,128]{2,1,0:T(8,128)} custom-call(bf16[128,32,128]{2,1,0:T(8,128)(2,1)S(1)} %all_to_all.23.y_ref, f32[4680,128]{1,0:T(8,128)S(1)} %get-tuple-element.21.z_ref, f32[4680,128]{1,0:T(8,128)S(1)} %get-tuple-element.22.gate_ref, f32[2,128]{1,0:T(2,128)S(1)} %copy-done.8, f32[2,128]{1,0:T(2,128)S(1)} %copy-done.9, ...), custom_call_target="tpu_custom_call" | custom-call | tf_op jit(solution)/shard_map/pallas_call | solution.py:365
  (5 shorter events, 0.0 us)
Async XLA Ops:
  75.1 2.7 %collective-permute-start = (bf16[1024,512]{1,0:T(8,128)(2,1)S(1)}, bf16[1024,512]{1,0:T(8,128)(2,1)S(1)}, u32[]{:S(2)}, u32[]{:S(2)}) collective-permute-start(bf16[1024,512]{1,0:T(8,128)(2,1)S(1)} %get-tuple-element.16), channel_id=1, source_target_pairs={{0,1},{1,0},{2,3},{3,2},{4,5},{5,4},{6,7},{7,6},{8,9},{9,8},{10,11... | collective-permute-start | bytes 3145736 | tf_op jit(solution)/shard_map/ppermute | solution.py:350
  77.9 38.6 %copy-start.1 = (f32[32,128,128]{2,1,0:T(8,128)S(1)}, f32[32,128,128]{2,1,0:T(8,128)}, u32[]{:S(2)}) copy-start(f32[32,128,128]{2,1,0:T(8,128)} %get-tuple-element.17.gate0_ref) | copy-start | bytes 6291460
  77.9 38.6 %copy-start.2 = (bf16[2,128,512]{2,1,0:T(8,128)(2,1)S(1)}, bf16[2,128,512]{2,1,0:T(8,128)(2,1)}, u32[]{:S(2)}) copy-start(bf16[2,128,512]{2,1,0:T(8,128)(2,1)} %w_ref.1) | copy-start | bytes 786436
  77.9 38.6 %copy-start.3 = (bf16[2,128,128]{2,1,0:T(8,128)(2,1)S(1)}, bf16[2,128,128]{2,1,0:T(8,128)(2,1)}, u32[]{:S(2)}) copy-start(bf16[2,128,128]{2,1,0:T(8,128)(2,1)} %g_ref.1) | copy-start | bytes 196612
  77.9 38.6 %copy-start.4 = (bf16[2,128,128]{2,1,0:T(8,128)(2,1)S(1)}, bf16[2,128,128]{2,1,0:T(8,128)(2,1)}, u32[]{:S(2)}) copy-start(bf16[2,128,128]{2,1,0:T(8,128)(2,1)} %ow_ref.3) | copy-start | bytes 196612
  77.9 38.6 %copy-start.5 = (s32[1024]{0:T(1024)S(1)}, s32[1024]{0:T(1024)}, u32[]{:S(2)}) copy-start(s32[1024]{0:T(1024)} %token_ref.1) | copy-start | bytes 12292
  77.9 38.6 %copy-start.7 = (f32[2,128]{1,0:T(2,128)S(1)}, f32[2,128]{1,0:T(2,128)}, u32[]{:S(2)}) copy-start(f32[2,128]{1,0:T(2,128)} %bias_ref.1) | copy-start | bytes 3076
  77.9 38.6 %copy-start.8 = (f32[2,128]{1,0:T(2,128)S(1)}, f32[2,128]{1,0:T(2,128)}, u32[]{:S(2)}) copy-start(f32[2,128]{1,0:T(2,128)} %mgain_ref.3) | copy-start | bytes 3076
  77.9 38.6 %copy-start.9 = (f32[2,128]{1,0:T(2,128)S(1)}, f32[2,128]{1,0:T(2,128)}, u32[]{:S(2)}) copy-start(f32[2,128]{1,0:T(2,128)} %mbias_ref.3) | copy-start | bytes 3076
  78.3 38.2 %copy-start = (f32[64,64,128]{2,1,0:T(8,128)S(1)}, f32[64,64,128]{2,1,0:T(8,128)}, u32[]{:S(2)}) copy-start(f32[64,64,128]{2,1,0:T(8,128)} %z_ref.1) | copy-start | bytes 6291460
  78.3 38.2 %copy-start.6 = (f32[2,128]{1,0:T(2,128)S(1)}, f32[2,128]{1,0:T(2,128)}, u32[]{:S(2)}) copy-start(f32[2,128]{1,0:T(2,128)} %gain_ref.1) | copy-start | bytes 3076
  181.1 2.7 %collective-permute-start.1 = (bf16[512,1024]{1,0:T(8,128)(2,1)S(1)}, bf16[512,1024]{1,0:T(8,128)(2,1)S(1)}, u32[]{:S(2)}, u32[]{:S(2)}) collective-permute-start(bf16[512,1024]{1,0:T(8,128)(2,1)S(1)} %shard_map.96.l_ref), channel_id=1, source_target_pairs={{0,1},{1,0},{2,3},{3,2},{4,5},{5,4},{6,7},{7,6},{8,9},{9,8},{10,11... | collective-permute-start | bytes 3145736 | tf_op jit(solution)/shard_map/ppermute | solution.py:361

commit v6 on v5

--- a/solution.py
+++ b/solution.py
@@ -73,9 +73,10 @@
         p = lax.dot_general(
             w, normed, (((0,), (1,)), ((), ())), preferred_element_type=F32
         )
-        gate = jnp.tanh(jnp.dot(normed, g, preferred_element_type=F32)) + 1.0
-        keep_gate(s, gate[:C])
-        keep_gate(s + 1, gate[C:])
+        if keep_gate is not None:
+            gate = jnp.tanh(jnp.dot(normed, g, preferred_element_type=F32)) + 1.0
+            keep_gate(s, gate[:C])
+            keep_gate(s + 1, gate[C:])
         left = (jnp.tanh(p[:C]) + 1.0) * p[C : 2 * C]
         right = (jnp.tanh(p[2 * C : 3 * C]) + 1.0) * p[3 * C :]
         for u in range(2):
@@ -87,15 +88,15 @@
 
 
 def first_kernel(
-    z_hbm, token_hbm, mask_hbm, gain_hbm, bias_hbm, w_hbm, g_hbm, x_hbm, gate_hbm, sl_ref, sr_ref,
-    z_ref, token_ref, mask_ref, gain_ref, bias_ref, w_ref, g_ref, x_ref, gate_ref, small_sem, z_sem, out_sem,
+    z_hbm, token_hbm, mask_hbm, gain_hbm, bias_hbm, w_hbm, x_hbm, sl_ref, sr_ref,
+    z_ref, token_ref, mask_ref, gain_ref, bias_ref, w_ref, x_ref, small_sem, z_sem, out_sem,
 ):
     small = [
         pltpu.make_async_copy(source, to, small_sem.at[n])
         for n, (source, to) in enumerate(
             (
                 (gain_hbm, gain_ref), (bias_hbm, bias_ref), (mask_hbm, mask_ref), (token_hbm, token_ref),
-                (w_hbm.at[0], w_ref), (g_hbm.at[0], g_ref),
+                (w_hbm.at[0], w_ref),
             )
         )
     ]
@@ -110,11 +111,8 @@
     gain, bias = gain_ref[0:1], bias_ref[0:1]
     across = lanes_twice(mask_ref, col_block())
     start = row_block() * T
-    w, g = gate_weights_halved(w_ref[...]), halved(g_ref[...])
+    w = gate_weights_halved(w_ref[...])
     copies = []
-
-    def keep_gate(s, value):
-        gate_ref[s] = value
 
     def send(source, to):
         copies.append(pltpu.make_async_copy(source, to, out_sem.at[len(copies)]))
@@ -125,15 +123,23 @@
         parts[2 * block + 1].wait()
         project_block(
             lambda s: z_ref[s], block, lambda s: line_mask(token_ref, start, s, across), gain, bias,
-            w, g, x_ref, keep_gate, sl_ref, sr_ref,
+            w, None, x_ref, None, sl_ref, sr_ref,
         )
         for half in range(2):
             lines = pl.ds(half * H + block * BLK, BLK)
             send(x_ref.at[:, lines], x_hbm.at[:, lines])
-        lines = pl.ds(block * BLK, BLK)
-        send(gate_ref.at[lines], gate_hbm.at[lines])
     for copy in copies:
         copy.wait()
+
+
+def gate_kernel(z_ref, gain_ref, bias_ref, g_ref, gate_ref):
+    gain, bias, g = gain_ref[0:1], bias_ref[0:1], halved(g_ref[0])
+    for s in range(0, H, 2):
+        lines = jnp.concatenate([z_ref[s], z_ref[s + H], z_ref[s + 1], z_ref[s + 1 + H]], axis=0)
+        normed = layer_norm(lines, gain, bias).astype(BF16)
+        gate = jnp.tanh(jnp.dot(normed, g, preferred_element_type=F32)) + 1.0
+        gate_ref[s] = gate[:C]
+        gate_ref[s + 1] = gate[C:]
 
 
 def update_block(block, y_ref, gain, bias, ow, s_ref, emit):
@@ -330,24 +336,26 @@
     line = (((C + 1) * PITCH, 2 * T), F32)
     tile = (((T + 1) * WIDE, C), F32)
 
-    x, gate0 = call(
+    (x,) = call(
         first_kernel,
-        [wide, gates],
+        [wide],
         [
             line, line, ((T, T, C), F32), pltpu.SMEM((1024,), jnp.int32), ((1, 1024), jnp.int32), ((2, C), F32),
-            ((2, C), F32), ((C, 4 * C), BF16), ((C, C), BF16), wide, gates, pltpu.SemaphoreType.DMA((6,)),
-            pltpu.SemaphoreType.DMA((T // BLK,)), pltpu.SemaphoreType.DMA((6,)),
+            ((2, C), F32), ((C, 4 * C), BF16), wide, pltpu.SemaphoreType.DMA((5,)),
+            pltpu.SemaphoreType.DMA((T // BLK,)), pltpu.SemaphoreType.DMA((4,)),
         ],
-        [HBM_SPEC] * 7,
-        [HBM_SPEC] * 2,
+        [HBM_SPEC] * 6,
+        [HBM_SPEC],
         FIRST_LIMIT,
     )(
-        pair, token_mask, mask, in_gain, in_bias, proj_weight, gate_weight
+        pair, token_mask, mask, in_gain, in_bias, proj_weight
     )
     x = exchange(x)
     right = ((512, 512), BF16)
     left, other = call(outgoing_other_kernel, [((1024, 512), BF16), ((1024, 512), BF16)], [right])(x)
     got = lax.ppermute(other, "core", SWAP)
+    later = lax.optimization_barrier((pair, other))[0]
+    (gate0,) = call(gate_kernel, [gates])(later, in_gain, in_bias, gate_weight)
     (own,) = call(outgoing_own_kernel, [((1024, 512), F32)], [right])(x, left)
     (y,) = call(outgoing_sum_kernel, [narrow])(own, got)
     y = exchange(y)

time: 226 us -> 229 us (1.013)
  blocking collectives: 203 us -> 165 us
  waiting for transfers between devices: 3.44 us -> 31.8 us
  starting transfers between devices: 0.19 us -> 6.74 us
  local copies, waits for them, and re-layouts: 0.05 us -> 4.59 us
    all_to_all x4 -> x3, blocking collectives: 203 us -> 165 us  [exchange(): return lax.all_to_all(x, CHIPS, split_axis=0, concat_axis=0, tiled=True)]
    all_to_all x0 -> x1, waiting for transfers between devices: none -> 28.4 us  [exchange(): return lax.all_to_all(x, CHIPS, split_axis=0, concat_axis=0, tiled=True)]
    all_to_all x0 -> x1, starting transfers between devices: none -> 6.56 us  [exchange(): return lax.all_to_all(x, CHIPS, split_axis=0, concat_axis=0, tiled=True)]
    unnamed x20 -> x24, local copies, waits for them, and re-layouts: 0.05 us -> 4.59 us
    pallas_call x1 -> x2, Pallas kernels: 5.74 us -> 7.16 us  [the longest x1 5.3 us: on_device(): call(first_kernel, [wide], [line, line, ((T, T, C), F32), pltpu.SMEM((102...]
  transfers between devices with their start and end apart: 2 -> 3, of which waited for: 2 -> 3; matrix products, arithmetic and copies ran while one was open for 0% -> 0% of each run, Pallas kernels for 1% -> 2%
where the time goes in v6:
time: 229 us; the launch traced here: 228 us
  blocking collectives  165 us (72%)
  waiting for transfers between devices  31.8 us (14%)
  Pallas kernels  20 us (9%)
  starting transfers between devices  6.74 us (3%)
  local copies, waits for them, and re-layouts  4.59 us (2%)
    all_to_all x3, blocking collectives, exchange(): return lax.all_to_all(x, CHIPS, split_axis=0, concat_axis=0, tiled=True)  165 us
    all_to_all x1, waiting for transfers between devices, exchange(): return lax.all_to_all(x, CHIPS, split_axis=0, concat_axis=0, tiled=True)  28.4 us
    all_to_all x1, starting transfers between devices, exchange(): return lax.all_to_all(x, CHIPS, split_axis=0, concat_axis=0, tiled=True)  6.56 us
    pallas_call x1, Pallas kernels, on_device(): call(middle_kernel, [wide, tile, tile], [line, line], [VMEM_SPEC] * 6 + [...  5.55 us
    pallas_call x1, Pallas kernels, on_device(): call(first_kernel, [wide], [line, line, ((T, T, C), F32), pltpu.SMEM((102...  5.3 us
    unnamed x24, local copies, waits for them, and re-layouts  4.59 us
  transfers between devices with their start and end apart: 3, of which 3 were waited for; matrix products, arithmetic and copies ran while one was open for 0% of the time, Pallas kernels for 2%

profile of v6, /device:TPU:32, one launch (start us, length us, event | category | flops | bytes accessed | tf_op | source)
XLA Modules:
  0.0 228.4 jit_solution(9591871191521779471)
XLA Ops:
  0.0 5.3 %shard_map.91 = bf16[128,64,128]{2,1,0:T(8,128)(2,1)} custom-call(f32[64,64,128]{2,1,0:T(8,128)} %z_ref.2, s32[1024]{0:T(1024)} %token_ref.1, s32[1,1024]{1,0:T(1,128)} %bitcast.1, f32[2,128]{1,0:T(2,128)} %gain_ref.3, f32[2,128]{1,0:T(2,128)} %bias_ref.3, bf16[2,128,512]{2,1,0:T(8,128)(2,1)} %w_ref.1), custom_call_target="tpu_custom_call" | custom-call | tf_op jit(solution)/shard_map/pallas_call | solution.py:339
  5.3 68.5 %all_to_all.20.x_ref = bf16[128,64,128]{2,1,0:T(8,128)(2,1)S(1)} all-to-all(bf16[128,64,128]{2,1,0:T(8,128)(2,1)} %shard_map.91), channel_id=1, replica_groups=mesh['z'=8,'yl'=2,'x'=4,'yh'=2,'core'=2] {'z','yh','yl','x'}, dimensions={0} | all-to-all | bytes 4194304 | tf_op jit(solution)/shard_map/all_to_all | solution.py:326
  73.8 0.9 shard_map.92
  74.7 0.1 collective-permute-start
  74.8 0.9 shard_map.93.own_ref
  75.7 1.8 collective-permute-done.got_ref
  77.4 0.3 shard_map.94
  77.8 0.0 copy-start.3
  77.8 1.0 copy-done.3
  78.8 6.6 %all-to-all-start.1 = ((bf16[128,32,128]{2,1,0:T(8,128)(2,1)}), bf16[128,32,128]{2,1,0:T(8,128)(2,1)S(1)}, u32[]{:S(2)}, u32[]{:S(2)}) async-start(bf16[128,32,128]{2,1,0:T(8,128)(2,1)} %copy-done.3), calls=%async_computation.1 | async-start | bytes 2097152 | tf_op jit(solution)/shard_map/all_to_all | solution.py:326
  85.3 0.0 copy-done.5
  85.4 0.0 copy-done.8
  85.4 0.0 copy-done.9
  85.4 0.0 copy-start.4
  85.4 0.0 copy-start.6
  85.4 0.0 copy-start.7
  85.4 0.0 copy-start.10
  85.4 1.9 shard_map.95.gate0_ref
  87.3 0.0 copy-start.1
  87.3 1.3 copy-done.1
  88.6 28.4 %all-to-all-done.1.y_ref = bf16[128,32,128]{2,1,0:T(8,128)(2,1)S(1)} async-done(((bf16[128,32,128]{2,1,0:T(8,128)(2,1)}), bf16[128,32,128]{2,1,0:T(8,128)(2,1)S(1)}, u32[]{:S(2)}, u32[]{:S(2)}) %all-to-all-start.1) | async-done | bytes 1048608 | tf_op jit(solution)/shard_map/all_to_all | solution.py:326
  117.0 1.6 copy-done.2
  118.6 0.7 copy-done.11
  119.3 5.5 %shard_map.96 = (bf16[128,64,128]{2,1,0:T(8,128)(2,1)S(1)}, f32[4680,128]{1,0:T(8,128)S(1)}, f32[4680,128]{1,0:T(8,128)S(1)}) custom-call(bf16[128,32,128]{2,1,0:T(8,128)(2,1)S(1)} %all-to-all-done.1.y_ref, f32[64,64,128]{2,1,0:T(8,128)S(1)} %copy-done, f32[32,128,128]{2,1,0:T(8,128)S(1)} %copy-done.2, f32[2,128]{1,0:T(2,128)S(1)} %copy-done.10, ...), custom_call_target="tpu_custom_call" | custom-call | tf_op jit(solution)/shard_map/pallas_call | solution.py:362
  124.8 58.7 %all_to_all.21.x_ref = bf16[128,64,128]{2,1,0:T(8,128)(2,1)S(1)} all-to-all(bf16[128,64,128]{2,1,0:T(8,128)(2,1)S(1)} %get-tuple-element.16), channel_id=1, replica_groups=mesh['z'=8,'yl'=2,'x'=4,'yh'=2,'core'=2] {'z','yh','yl','x'}, dimensions={0} | all-to-all | bytes 4194304 | tf_op jit(solution)/shard_map/all_to_all | solution.py:326
  183.5 0.3 shard_map.97.l_ref
  183.8 0.1 collective-permute-start.1
  183.9 1.0 shard_map.98
  184.9 1.7 collective-permute-done.1.l_ref
  186.6 0.8 shard_map.99
  187.4 37.8 %all_to_all.22.y_ref = bf16[128,32,128]{2,1,0:T(8,128)(2,1)S(1)} all-to-all(bf16[128,32,128]{2,1,0:T(8,128)(2,1)S(1)} %shard_map.99), channel_id=1, replica_groups=mesh['z'=8,'yl'=2,'x'=4,'yh'=2,'core'=2] {'z','yh','yl','x'}, dimensions={0} | all-to-all | bytes 2097152 | tf_op jit(solution)/shard_map/all_to_all | solution.py:326
  225.3 3.0 %shard_map.100 = f32[64,64,128]{2,1,0:T(8,128)} custom-call(bf16[128,32,128]{2,1,0:T(8,128)(2,1)S(1)} %all_to_all.22.y_ref, f32[4680,128]{1,0:T(8,128)S(1)} %get-tuple-element.19.z_ref, f32[4680,128]{1,0:T(8,128)S(1)} %get-tuple-element.20.gate_ref, f32[2,128]{1,0:T(2,128)S(1)} %copy-done.10, f32[2,128]{1,0:T(2,128)S(1)} %copy-done.11, ...), custom_call_target="tpu_custom_call" | custom-call | tf_op jit(solution)/shard_map/pallas_call | solution.py:373
  (11 shorter events, 0.0 us)
Async XLA Ops:
  74.7 2.7 %collective-permute-start = (bf16[1024,512]{1,0:T(8,128)(2,1)S(1)}, bf16[1024,512]{1,0:T(8,128)(2,1)S(1)}, u32[]{:S(2)}, u32[]{:S(2)}) collective-permute-start(bf16[1024,512]{1,0:T(8,128)(2,1)S(1)} %get-tuple-element.14), channel_id=1, source_target_pairs={{0,1},{1,0},{2,3},{3,2},{4,5},{5,4},{6,7},{7,6},{8,9},{9,8},{10,11... | collective-permute-start | bytes 3145736 | tf_op jit(solution)/shard_map/ppermute | solution.py:356
  77.4 7.9 %copy-start.5 = (bf16[2,128,128]{2,1,0:T(8,128)(2,1)S(1)}, bf16[2,128,128]{2,1,0:T(8,128)(2,1)}, u32[]{:S(2)}) copy-start(bf16[2,128,128]{2,1,0:T(8,128)(2,1)} %g_ref.3) | copy-start | bytes 196612
  77.4 7.9 %copy-start.8 = (f32[2,128]{1,0:T(2,128)S(1)}, f32[2,128]{1,0:T(2,128)}, u32[]{:S(2)}) copy-start(f32[2,128]{1,0:T(2,128)} %gain_ref.3) | copy-start | bytes 3076
  77.4 7.9 %copy-start.9 = (f32[2,128]{1,0:T(2,128)S(1)}, f32[2,128]{1,0:T(2,128)}, u32[]{:S(2)}) copy-start(f32[2,128]{1,0:T(2,128)} %bias_ref.3) | copy-start | bytes 3076
  77.8 1.0 copy-start.3
  78.8 6.6 %copy-start = (f32[64,64,128]{2,1,0:T(8,128)S(1)}, f32[64,64,128]{2,1,0:T(8,128)}, u32[]{:S(2)}) copy-start(f32[64,64,128]{2,1,0:T(8,128)} %z_ref.2) | copy-start | bytes 6291460
  78.8 38.2 %all-to-all-start.1 = ((bf16[128,32,128]{2,1,0:T(8,128)(2,1)}), bf16[128,32,128]{2,1,0:T(8,128)(2,1)S(1)}, u32[]{:S(2)}, u32[]{:S(2)}) async-start(bf16[128,32,128]{2,1,0:T(8,128)(2,1)} %copy-done.3), calls=%async_computation.1 | async-start | bytes 2097152 | tf_op jit(solution)/shard_map/all_to_all | solution.py:326
  85.4 31.6 %copy-start.4 = (bf16[2,128,512]{2,1,0:T(8,128)(2,1)S(1)}, bf16[2,128,512]{2,1,0:T(8,128)(2,1)}, u32[]{:S(2)}) copy-start(bf16[2,128,512]{2,1,0:T(8,128)(2,1)} %w_ref.1) | copy-start | bytes 786436
  85.4 31.6 %copy-start.6 = (bf16[2,128,128]{2,1,0:T(8,128)(2,1)S(1)}, bf16[2,128,128]{2,1,0:T(8,128)(2,1)}, u32[]{:S(2)}) copy-start(bf16[2,128,128]{2,1,0:T(8,128)(2,1)} %ow_ref.3) | copy-start | bytes 196612
  85.4 31.6 %copy-start.7 = (s32[1024]{0:T(1024)S(1)}, s32[1024]{0:T(1024)}, u32[]{:S(2)}) copy-start(s32[1024]{0:T(1024)} %token_ref.1) | copy-start | bytes 12292
  85.4 31.6 %copy-start.10 = (f32[2,128]{1,0:T(2,128)S(1)}, f32[2,128]{1,0:T(2,128)}, u32[]{:S(2)}) copy-start(f32[2,128]{1,0:T(2,128)} %mgain_ref.3) | copy-start | bytes 3076
  87.3 1.3 copy-start.1
  117.0 1.6 copy-start.2
  118.6 0.7 copy-start.11
  183.8 2.7 %collective-permute-start.1 = (bf16[512,1024]{1,0:T(8,128)(2,1)S(1)}, bf16[512,1024]{1,0:T(8,128)(2,1)S(1)}, u32[]{:S(2)}, u32[]{:S(2)}) collective-permute-start(bf16[512,1024]{1,0:T(8,128)(2,1)S(1)} %shard_map.97.l_ref), channel_id=1, source_target_pairs={{0,1},{1,0},{2,3},{3,2},{4,5},{5,4},{6,7},{7,6},{8,9},{9,8},{10,11... | collective-permute-start | bytes 3145736 | tf_op jit(solution)/shard_map/ppermute | solution.py:369

commit v7 on v5

--- a/solution.py
+++ b/solution.py
@@ -66,20 +66,17 @@
 
 
 def project_block(load, block, mask, gain, bias, w, g, x_ref, keep_gate, sl_ref, sr_ref):
-    for t in range(0, BLK, 2):
+    for t in range(0, BLK, 4):
         s = block * BLK + t
-        lines = jnp.concatenate([load(s), load(s + H), load(s + 1), load(s + 1 + H)], axis=0)
+        lines = jnp.concatenate([load(s + u + h) for u in range(4) for h in (0, H)], axis=0)
         normed = layer_norm(lines, gain, bias).astype(BF16)
-        p = lax.dot_general(
-            w, normed, (((0,), (1,)), ((), ())), preferred_element_type=F32
-        )
+        p = lax.dot_general(w, normed, (((0,), (1,)), ((), ())), preferred_element_type=F32)
         gate = jnp.tanh(jnp.dot(normed, g, preferred_element_type=F32)) + 1.0
-        keep_gate(s, gate[:C])
-        keep_gate(s + 1, gate[C:])
         left = (jnp.tanh(p[:C]) + 1.0) * p[C : 2 * C]
         right = (jnp.tanh(p[2 * C : 3 * C]) + 1.0) * p[3 * C :]
-        for u in range(2):
+        for u in range(4):
             keep = mask(s + u)
+            keep_gate(s + u, gate[u * C : (u + 1) * C])
             sl_ref[pl.ds(t + u, C, stride=PITCH), :] = left[:, u * C : (u + 1) * C] * keep
             sr_ref[pl.ds(t + u, C, stride=PITCH), :] = right[:, u * C : (u + 1) * C] * keep
     x_ref[:, pl.ds(pl.multiple_of(block * BLK, BLK), BLK), :] = unpad(sl_ref)

time: 226 us -> 226 us (level)
  no operation moved by 1% of the time
where the time goes in v7:
time: 226 us
  blocking collectives  203 us (90%)
  Pallas kernels  18.7 us (8%)
  waiting for transfers between devices  3.44 us (2%)
    all_to_all x4, blocking collectives, exchange(): return lax.all_to_all(x, CHIPS, split_axis=0, concat_axis=0, tiled=True)  203 us
    pallas_call x1, Pallas kernels, on_device(): call(first_kernel, [wide, gates], [line, line, ((T, T, C), F32), pltpu.SM...  5.84 us
    pallas_call x1, Pallas kernels, on_device(): call(middle_kernel, [wide, tile, tile], [line, line], [VMEM_SPEC] * 6 + [...  5.61 us
  transfers between devices with their start and end apart: 2, of which 2 were waited for; matrix products, arithmetic and copies ran while one was open for 0% of the time, Pallas kernels for 1%

profile of v7, /device:TPU:32, one launch (start us, length us, event | category | flops | bytes accessed | tf_op | source)
XLA Modules:
  0.0 225.8 jit_solution(3562702032866714211)
XLA Ops:
  0.0 5.8 %shard_map.91 = (bf16[128,64,128]{2,1,0:T(8,128)(2,1)}, f32[32,128,128]{2,1,0:T(8,128)}) custom-call(f32[64,64,128]{2,1,0:T(8,128)} %z_ref.1, s32[1024]{0:T(1024)} %token_ref.1, s32[1,1024]{1,0:T(1,128)} %bitcast.1, f32[2,128]{1,0:T(2,128)} %gain_ref.1, f32[2,128]{1,0:T(2,128)} %bias_ref.1, bf16[2,128,512]{2,1,0:T(8,128)(2,1)} %w_ref.1, ...), custom_call_target="tpu_custom_call" | custom-call | tf_op jit(solution)/shard_map/pallas_call | solution.py:330
  5.8 68.5 %all_to_all.20.x_ref = bf16[128,64,128]{2,1,0:T(8,128)(2,1)S(1)} all-to-all(bf16[128,64,128]{2,1,0:T(8,128)(2,1)} %get-tuple-element.14), channel_id=1, replica_groups=mesh['z'=8,'yl'=2,'x'=4,'yh'=2,'core'=2] {'z','yh','yl','x'}, dimensions={0} | all-to-all | bytes 4194304 | tf_op jit(solution)/shard_map/all_to_all | solution.py:317
  74.3 0.9 shard_map.92
  75.2 0.1 collective-permute-start
  75.3 0.9 shard_map.93.own_ref
  76.2 1.8 collective-permute-done.got_ref
  78.0 0.0 copy-start.5
  78.0 0.0 copy-start.7
  78.0 0.0 copy-start.8
  78.0 0.0 copy-start.9
  78.0 0.3 shard_map.94
  78.4 0.0 copy-start
  78.4 0.0 copy-start.6
  78.4 38.1 %all_to_all.21.y_ref = bf16[128,32,128]{2,1,0:T(8,128)(2,1)S(1)} all-to-all(bf16[128,32,128]{2,1,0:T(8,128)(2,1)S(1)} %shard_map.94), channel_id=1, replica_groups=mesh['z'=8,'yl'=2,'x'=4,'yh'=2,'core'=2] {'z','yh','yl','x'}, dimensions={0} | all-to-all | bytes 2097152 | tf_op jit(solution)/shard_map/all_to_all | solution.py:317
  116.5 0.0 copy-done.1
  116.5 0.0 copy-done.2
  116.5 0.0 copy-done.3
  116.5 0.0 copy-done.4
  116.5 0.0 copy-done.5
  116.6 0.0 copy-done.7
  116.6 0.0 copy-done.8
  116.6 0.0 copy-done.9
  116.6 0.0 copy-done
  116.6 5.6 %shard_map.95 = (bf16[128,64,128]{2,1,0:T(8,128)(2,1)S(1)}, f32[4680,128]{1,0:T(8,128)S(1)}, f32[4680,128]{1,0:T(8,128)S(1)}) custom-call(bf16[128,32,128]{2,1,0:T(8,128)(2,1)S(1)} %all_to_all.21.y_ref, f32[64,64,128]{2,1,0:T(8,128)S(1)} %copy-done, f32[32,128,128]{2,1,0:T(8,128)S(1)} %copy-done.1, f32[2,128]{1,0:T(2,128)S(1)} %copy-done.8, ...), custom_call_target="tpu_custom_call" | custom-call | tf_op jit(solution)/shard_map/pallas_call | solution.py:351
  122.2 58.7 %all_to_all.22.x_ref = bf16[128,64,128]{2,1,0:T(8,128)(2,1)S(1)} all-to-all(bf16[128,64,128]{2,1,0:T(8,128)(2,1)S(1)} %get-tuple-element.18), channel_id=1, replica_groups=mesh['z'=8,'yl'=2,'x'=4,'yh'=2,'core'=2] {'z','yh','yl','x'}, dimensions={0} | all-to-all | bytes 4194304 | tf_op jit(solution)/shard_map/all_to_all | solution.py:317
  180.9 0.3 shard_map.96.l_ref
  181.2 0.1 collective-permute-start.1
  181.3 1.0 shard_map.97
  182.3 1.7 collective-permute-done.1.l_ref
  184.0 0.8 shard_map.98
  184.8 37.8 %all_to_all.23.y_ref = bf16[128,32,128]{2,1,0:T(8,128)(2,1)S(1)} all-to-all(bf16[128,32,128]{2,1,0:T(8,128)(2,1)S(1)} %shard_map.98), channel_id=1, replica_groups=mesh['z'=8,'yl'=2,'x'=4,'yh'=2,'core'=2] {'z','yh','yl','x'}, dimensions={0} | all-to-all | bytes 2097152 | tf_op jit(solution)/shard_map/all_to_all | solution.py:317
  222.7 3.0 %shard_map.99 = f32[64,64,128]{2,1,0:T(8,128)} custom-call(bf16[128,32,128]{2,1,0:T(8,128)(2,1)S(1)} %all_to_all.23.y_ref, f32[4680,128]{1,0:T(8,128)S(1)} %get-tuple-element.21.z_ref, f32[4680,128]{1,0:T(8,128)S(1)} %get-tuple-element.22.gate_ref, f32[2,128]{1,0:T(2,128)S(1)} %copy-done.8, f32[2,128]{1,0:T(2,128)S(1)} %copy-done.9, ...), custom_call_target="tpu_custom_call" | custom-call | tf_op jit(solution)/shard_map/pallas_call | solution.py:362
  (5 shorter events, 0.0 us)
Async XLA Ops:
  75.2 2.7 %collective-permute-start = (bf16[1024,512]{1,0:T(8,128)(2,1)S(1)}, bf16[1024,512]{1,0:T(8,128)(2,1)S(1)}, u32[]{:S(2)}, u32[]{:S(2)}) collective-permute-start(bf16[1024,512]{1,0:T(8,128)(2,1)S(1)} %get-tuple-element.16), channel_id=1, source_target_pairs={{0,1},{1,0},{2,3},{3,2},{4,5},{5,4},{6,7},{7,6},{8,9},{9,8},{10,11... | collective-permute-start | bytes 3145736 | tf_op jit(solution)/shard_map/ppermute | solution.py:347
  78.0 38.6 %copy-start.1 = (f32[32,128,128]{2,1,0:T(8,128)S(1)}, f32[32,128,128]{2,1,0:T(8,128)}, u32[]{:S(2)}) copy-start(f32[32,128,128]{2,1,0:T(8,128)} %get-tuple-element.17.gate0_ref) | copy-start | bytes 6291460
  78.0 38.6 %copy-start.2 = (bf16[2,128,512]{2,1,0:T(8,128)(2,1)S(1)}, bf16[2,128,512]{2,1,0:T(8,128)(2,1)}, u32[]{:S(2)}) copy-start(bf16[2,128,512]{2,1,0:T(8,128)(2,1)} %w_ref.1) | copy-start | bytes 786436
  78.0 38.6 %copy-start.3 = (bf16[2,128,128]{2,1,0:T(8,128)(2,1)S(1)}, bf16[2,128,128]{2,1,0:T(8,128)(2,1)}, u32[]{:S(2)}) copy-start(bf16[2,128,128]{2,1,0:T(8,128)(2,1)} %g_ref.1) | copy-start | bytes 196612
  78.0 38.6 %copy-start.4 = (bf16[2,128,128]{2,1,0:T(8,128)(2,1)S(1)}, bf16[2,128,128]{2,1,0:T(8,128)(2,1)}, u32[]{:S(2)}) copy-start(bf16[2,128,128]{2,1,0:T(8,128)(2,1)} %ow_ref.3) | copy-start | bytes 196612
  78.0 38.6 %copy-start.5 = (s32[1024]{0:T(1024)S(1)}, s32[1024]{0:T(1024)}, u32[]{:S(2)}) copy-start(s32[1024]{0:T(1024)} %token_ref.1) | copy-start | bytes 12292
  78.0 38.6 %copy-start.7 = (f32[2,128]{1,0:T(2,128)S(1)}, f32[2,128]{1,0:T(2,128)}, u32[]{:S(2)}) copy-start(f32[2,128]{1,0:T(2,128)} %bias_ref.1) | copy-start | bytes 3076
  78.0 38.6 %copy-start.8 = (f32[2,128]{1,0:T(2,128)S(1)}, f32[2,128]{1,0:T(2,128)}, u32[]{:S(2)}) copy-start(f32[2,128]{1,0:T(2,128)} %mgain_ref.3) | copy-start | bytes 3076
  78.0 38.6 %copy-start.9 = (f32[2,128]{1,0:T(2,128)S(1)}, f32[2,128]{1,0:T(2,128)}, u32[]{:S(2)}) copy-start(f32[2,128]{1,0:T(2,128)} %mbias_ref.3) | copy-start | bytes 3076
  78.4 38.2 %copy-start = (f32[64,64,128]{2,1,0:T(8,128)S(1)}, f32[64,64,128]{2,1,0:T(8,128)}, u32[]{:S(2)}) copy-start(f32[64,64,128]{2,1,0:T(8,128)} %z_ref.1) | copy-start | bytes 6291460
  78.4 38.2 %copy-start.6 = (f32[2,128]{1,0:T(2,128)S(1)}, f32[2,128]{1,0:T(2,128)}, u32[]{:S(2)}) copy-start(f32[2,128]{1,0:T(2,128)} %gain_ref.1) | copy-start | bytes 3076
  181.2 2.7 %collective-permute-start.1 = (bf16[512,1024]{1,0:T(8,128)(2,1)S(1)}, bf16[512,1024]{1,0:T(8,128)(2,1)S(1)}, u32[]{:S(2)}, u32[]{:S(2)}) collective-permute-start(bf16[512,1024]{1,0:T(8,128)(2,1)S(1)} %shard_map.96.l_ref), channel_id=1, source_target_pairs={{0,1},{1,0},{2,3},{3,2},{4,5},{5,4},{6,7},{7,6},{8,9},{9,8},{10,11... | collective-permute-start | bytes 3145736 | tf_op jit(solution)/shard_map/ppermute | solution.py:358
